TPU v7x, 32 devices: a whole 2x2x4 slice. The times are simulated.
32 devices in a mesh: span: 8 (over z, x), elem: 4 (over y, core).
Axes of the slice: x: 2, y: 2, z: 4, core: 2. Of those that a mesh axis runs over, the one named last changes fastest.
Arguments:
- species: float32 [81, 3, 512, 512], P(None, None, 'span', 'elem'), may hold values from 0.02 to 0.3
- laplacian: float32 [81, 3, 512, 512], P(None, None, 'span', 'elem'), may hold values from -6 to 6
- binary: float32 [3, 4], replicated, may hold values from 0.3 to 3
- dref: float32 [3], replicated, may hold values from 0.5 to 2
- stiff_eig: float32 [9], replicated, may hold values from 0.02 to 3
- basis: float32 [9, 9], replicated, may hold values from -1 to 1, as said below
- rounds: int32 [256], replicated, may hold values from 1 to 4
- adjacency: int32 [512, 4], P('elem'), may hold values from 0 to 511, as said below
- edge_map: int32 [512, 4], P('elem'), may hold values from 0 to 3
Outputs:
- updated: float32 [81, 3, 512, 512], P(None, None, 'span', 'elem')
Inputs may be any that keep to these rules, and one draw needn't show every extreme that they name: basis is an orthogonal matrix. The elements form a periodic mesh of 16 columns and 8 * 4 rows; each index of elem holds 8 whole rows in some order. adjacency is symmetric: element e lies across edge edge_map[e, j] of element adjacency[e, j]. The element across an edge lies on the same index of elem or on the one just before or after it, cyclically; exactly 16 elements of each index have an edge facing the next index and 16 one facing the previous, one such edge each.
All inputs are finite; a program needn't handle non-finite values.
Results may differ from a plain program's by a relative error of at most 0.0001.
Values sent between devices are 32-bit elements; how exact they have to be, the bound alone decides.
No kernel may reach another device: no remote copies, remote signals or barrier semaphores. Data moves between devices by JAX's collectives and lax.ppermute only.
A program may use at most 128 MiB of HBM per device.

v0:
```python
import jax
import jax.numpy as jnp
import numpy as np
from jax import lax
from jax.sharding import PartitionSpec as P

MESH_X = 16


coupling = 0.2
highest = lax.Precision.HIGHEST
two_pi = 6.283185307179586


def from_behind(block, axis, distance):
    devices = range(lax.axis_size(axis))
    route = [((i - distance) % len(devices), i) for i in devices]
    return lax.ppermute(block, axis, route)


def edge_lists(per_side):
    last_node = per_side - 1
    bottom = [i for i in range(per_side)]
    right_edge = [i * per_side + last_node for i in range(per_side)]
    top_edge = [last_node * per_side + last_node - i for i in range(per_side)]
    left_edge = [(last_node - i) * per_side for i in range(per_side)]
    return [bottom, right_edge, top_edge, left_edge]


def edge_matrix(per_side):
    edge_table = np.zeros((4, per_side, per_side * per_side), np.float32)
    for edge_id, node_list in enumerate(edge_lists(per_side)):
        for i, node_id in enumerate(node_list):
            edge_table[edge_id, i, node_id] = 1.0
    return edge_table


def mixture_source(species, laplacian, binary, dref):
    n_species = species.shape[1]
    bath_share = 1.0 - jnp.sum(species, axis=1)
    source_parts = []
    for s in range(n_species):
        resistance = bath_share / binary[s, n_species]
        for j in range(n_species):
            if j != s:
                resistance = resistance + species[:, j] / binary[s, j]
        mixture = (1.0 - species[:, s]) / resistance
        source_parts.append((species[:, s] + (mixture - dref[s]) * laplacian[:, s]) / dref[s])
    return jnp.stack(source_parts, axis=1)


def block_inverse(values, kron_basis, inverse_diag):
    n_nodes = values.shape[0]
    inner_part = (
        jnp.dot(kron_basis.T, values.reshape(n_nodes, -1), precision=highest).reshape(values.shape)
        * inverse_diag
    )
    return jnp.dot(kron_basis, inner_part.reshape(n_nodes, -1), precision=highest).reshape(
        values.shape
    )


def transform_tables(col_mode, col_part, planes):
    plane_ids = jnp.arange(planes, dtype=jnp.int32)
    phase_id = plane_ids[:, None] * col_mode[None, :] % planes
    angles = phase_id.astype(jnp.float32) * (two_pi / planes)
    trig_table = jnp.where(col_part[None, :] == 0, jnp.cos(angles), -jnp.sin(angles))
    weights = jnp.where(col_mode == 0, 1.0, 2.0).astype(jnp.float32)
    return (trig_table / planes, (trig_table * weights[None, :]).T)


def body(species, laplacian, binary, dref, stiff_eig, basis, rounds, adjacency, edge_map):
    per_side = basis.shape[0]
    n_nodes = per_side * per_side
    n_span = lax.axis_size("span")
    n_elem = lax.axis_size("elem")
    planes = species.shape[2] * n_span
    n_modes = planes // 2
    per_device = n_modes // n_span
    half_tile = per_device // 2
    own_count = adjacency.shape[0]
    source = mixture_source(species, laplacian, binary, dref)
    assign = jnp.arange(n_modes, dtype=jnp.int32).reshape(n_span, per_device)
    tile_count = 1
    col_mode = jnp.broadcast_to(
        assign.reshape(n_span, 2, 1, half_tile), (n_span, 2, 2, half_tile)
    ).reshape(planes)
    col_part = jnp.broadcast_to(
        jnp.arange(2, dtype=jnp.int32).reshape(1, 1, 2, 1), (n_span, 2, 2, half_tile)
    ).reshape(planes)
    forward, backward = transform_tables(col_mode, col_part, planes)
    source_swapped = jnp.transpose(source, (0, 1, 3, 2))
    coeffs = jnp.einsum(
        "nsez,zr->nser",
        lax.all_to_all(source_swapped, "span", split_axis=2, concat_axis=3, tiled=True),
        forward,
        precision=highest,
    )
    exchanged = lax.all_to_all(coeffs, "span", split_axis=3, concat_axis=2, tiled=True)
    modal_rhs = jnp.transpose(exchanged, (0, 1, 3, 2))
    columns = 2 * per_device
    my_modes = lax.dynamic_slice_in_dim(col_mode, lax.axis_index("span") * columns, columns)
    my_rounds = rounds[my_modes]
    wavenumber = my_modes.astype(jnp.float32) * (8.0 / planes)
    shifts = 1.0 / dref[:, None] + (wavenumber * wavenumber)[None, :]
    eig_sum = (stiff_eig[:, None] + stiff_eig[None, :]).reshape(n_nodes)
    inverse_diag = 1.0 / (shifts[None, :, :, None] + eig_sum[:, None, None, None])
    kron_basis = (basis[:, None, :, None] * basis[None, :, None, :]).reshape(n_nodes, n_nodes)
    flat_index = np.array(edge_lists(per_side)).reshape(-1)
    scatter_table = jnp.asarray(edge_matrix(per_side))
    owners = adjacency // own_count
    offset = (owners - lax.axis_index("elem") + n_elem) % n_elem
    local_id = adjacency % own_count
    flat_adj = adjacency.reshape(-1)
    flat_offset = offset.reshape(-1)
    earlier = flat_adj[None, :] < flat_adj[:, None]
    from_prev = flat_offset == n_elem - 1
    from_next = flat_offset == 1
    rank_prev = jnp.sum((earlier & from_prev[None, :]).astype(jnp.int32), axis=1)
    rank_next = jnp.sum((earlier & from_next[None, :]).astype(jnp.int32), axis=1)
    position = jnp.where(
        from_prev,
        own_count + rank_prev,
        jnp.where(from_next, own_count + MESH_X + rank_next, local_id.reshape(-1)),
    ).reshape(adjacency.shape)
    slot_ids = jnp.arange(MESH_X, dtype=jnp.int32)
    faces_next = jnp.any(offset == 1, axis=1)
    faces_prev = jnp.any(offset == n_elem - 1, axis=1)
    slot_next = jnp.cumsum(faces_next.astype(jnp.int32)) - 1
    slot_prev = jnp.cumsum(faces_prev.astype(jnp.int32)) - 1
    pick_next = (faces_next[:, None] & (slot_next[:, None] == slot_ids[None, :])).astype(
        jnp.float32
    )
    pick_prev = (faces_prev[:, None] & (slot_prev[:, None] == slot_ids[None, :])).astype(
        jnp.float32
    )

    def gather_pool(traces):
        send_up = jnp.einsum("ktsce,ea->ktsca", traces, pick_next, precision=highest)
        send_down = jnp.einsum("ktsce,ea->ktsca", traces, pick_prev, precision=highest)
        from_before = from_behind(send_up, "elem", 1)
        from_after = from_behind(send_down, "elem", -1)
        return jnp.concatenate([traces, from_before, from_after], axis=4)

    def couple(modal_field):
        traces = modal_field[flat_index].reshape((4, per_side) + modal_field.shape[1:])
        across = gather_pool(traces)[edge_map, :, :, :, position][:, :, ::-1]
        return jnp.einsum("jtn,ejtsc->nsce", scatter_table, across, precision=highest)

    tile_modes = assign.reshape(n_span, tile_count, per_device // tile_count)
    sweep_bound = jnp.max(rounds[tile_modes[:, 0].reshape(-1)])
    initial = block_inverse(modal_rhs, kron_basis, inverse_diag)

    def sweep_once(sweep_id, modal_field):
        proposal = block_inverse(
            modal_rhs + coupling * couple(modal_field), kron_basis, inverse_diag
        )
        return jnp.where(sweep_id < my_rounds[:, None], proposal, modal_field)

    solved = lax.fori_loop(1, sweep_bound, sweep_once, initial)
    solution_swapped = jnp.transpose(solved, (0, 1, 3, 2))
    values = jnp.einsum(
        "nser,rz->nsez",
        lax.all_to_all(solution_swapped, "span", split_axis=2, concat_axis=3, tiled=True),
        backward,
        precision=highest,
    )
    returned = lax.all_to_all(values, "span", split_axis=3, concat_axis=2, tiled=True)
    return jnp.transpose(returned, (0, 1, 3, 2))


def solution(mesh):
    return jax.shard_map(
        body,
        mesh=mesh,
        in_specs=(
            P(None, None, "span", "elem"),
            P(None, None, "span", "elem"),
            P(),
            P(),
            P(),
            P(),
            P(),
            P("elem", None),
            P("elem", None),
        ),
        out_specs=P(None, None, "span", "elem"),
        check_vma=False,
    )
```

profile of v0, /device:TPU:0, one launch (start us, length us, event | category | flops | bytes accessed | tf_op | source)
XLA Modules:
  0.0 1935.9 jit_solution(11416443359650860732)
XLA Ops:
  7.8 9.5 fusion.35
  17.4 7.3 fusion.39
  28.4 11.1 copy.174
  47.0 272.8 %all-to-all-done = f32[81,3,128,64]{0,3,1,2:T(8,128)} async-done(((f32[81,3,128,64]{0,3,1,2:T(8,128)}), f32[81,3,128,64]{0,3,1,2:T(8,128)}, u32[]{:S(2)}, u32[]{:S(2)}) %all-to-all-start) | async-done | bytes 7962656 | tf_op jit(solution)/shard_map/all_to_all | solution.py:95
  319.9 18.4 copy.176
  338.3 13.9 all_to_all.55
  352.2 25.4 %fusion.55 = f32[81,3,16,512]{3,2,1,0:T(8,128)} fusion(f32[81,3,16,512]{3,2,1,0:T(8,128)} %all_to_all.55, s32[512]{0:T(512)S(1)} %mul.128, pred[512]{0:T(512)(128)(4,1)S(1)} %eq.89), kind=kOutput, calls=%fused_computation.83 | convolution fusion | flops 12235046912 | bytes 15927808 | tf_op jit(solution)/shard_map/nsez,zr->nser/dot_general | solution.py:93
  377.6 11.2 copy.177
  403.8 262.7 %all-to-all-done.1 = f32[81,3,16,512]{0,2,1,3:T(8,128)} async-done(((f32[81,3,16,512]{0,2,1,3:T(8,128)}), f32[81,3,16,512]{0,2,1,3:T(8,128)}, u32[]{:S(2)}, u32[]{:S(2)}) %all-to-all-start.1) | async-done | bytes 7962656 | tf_op jit(solution)/shard_map/all_to_all | solution.py:99
  666.6 13.8 copy.179
  680.4 11.3 copy.180
  691.7 11.6 copy.197
  703.3 12.1 broadcast_multiply_fusion.1
  717.0 12.1 fusion.28
  733.8 536.5 %while.12 = (s32[]{:T(128)}, f32[81,3,64,128]{3,2,1,0:T(8,128)}, s32[]{:T(128)}, s32[64]{0:T(128)}, s32[128,4]{1,0:T(8,128)}, /*index=5*/s32[128,4]{1,0:T(8,128)...) while((s32[]{:T(128)}, f32[81,3,64,128]{3,2,1,0:T(8,128)}, ...), condition=%wide.region_9.10_spmd.clone.clone, body=%wide.region_8.9_spmd.sunk.clone.clone.sunk | while | flops 5079768064 | bytes 306081504 | solution.py:160
  739.9 7.7 copy.257
  747.7 8.4 copy.258
  756.1 9.9 fusion.122
  765.9 9.9 fusion.123
  780.3 9.1 copy.256
  792.7 10.2 pad_maximum_fusion.2
  802.8 17.9 gather_fusion.1
  820.7 7.3 copy.261
  834.6 10.5 copy.262
  845.1 11.0 bitcast_add_fusion.2
  864.9 9.2 copy.264
  874.1 10.5 fusion.125
  884.6 7.9 fusion.126
  897.7 11.7 broadcast_select_fusion.2
  914.4 7.7 copy.257
  922.1 8.4 copy.258
  930.5 9.9 fusion.122
  941.6 9.9 fusion.123
  955.8 9.1 copy.256
  968.2 10.2 pad_maximum_fusion.2
  978.3 17.6 gather_fusion.1
  1009.9 10.5 copy.262
  1020.4 11.0 bitcast_add_fusion.2
  1040.2 9.2 copy.264
  1049.4 10.8 fusion.125
  1060.1 7.9 fusion.126
  1073.2 11.7 broadcast_select_fusion.2
  1089.8 7.7 copy.257
  1097.5 8.4 copy.258
  1105.9 9.9 fusion.122
  1117.5 9.9 fusion.123
  1131.7 9.1 copy.256
  1144.0 10.2 pad_maximum_fusion.2
  1154.2 17.6 gather_fusion.1
  1185.7 10.5 copy.262
  1196.2 11.0 bitcast_add_fusion.2
  1216.0 9.2 copy.264
  1225.2 10.8 fusion.125
  1236.0 7.9 fusion.126
  1249.0 11.7 broadcast_select_fusion.2
  1270.3 11.1 copy.198
  1287.0 274.2 %all-to-all-done.2 = f32[81,3,128,64]{0,3,1,2:T(8,128)} async-done(((f32[81,3,128,64]{0,3,1,2:T(8,128)}), f32[81,3,128,64]{0,3,1,2:T(8,128)}, u32[]{:S(2)}, u32[]{:S(2)}) %all-to-all-start.2) | async-done | bytes 7962656 | tf_op jit(solution)/shard_map/all_to_all | solution.py:164
  1561.1 18.4 copy.200
  1579.6 13.9 all_to_all.63
  1593.4 25.5 %fusion.53 = f32[81,3,16,512]{3,2,1,0:T(8,128)} fusion(f32[81,3,16,512]{3,2,1,0:T(8,128)} %all_to_all.63, f32[512]{0:T(512)S(1)} %compare_select_fusion.3, s32[512]{0:T(512)S(1)} %copy-done.10, pred[512]{0:T(512)(128)(4,1)S(1)} %copy-done.17), kind=kOutput, calls=%fused_computation.81 | convolution fusion | flops 12235046912 | bytes 15929856 | tf_op jit(solution)/shard_map/nser,rz->nsez/dot_general | solution.py:162
  1618.9 11.1 copy.201
  1630.0 280.5 %all_to_all.72 = f32[81,3,16,512]{0,2,1,3:T(8,128)} all-to-all(f32[81,3,16,512]{0,2,1,3:T(8,128)} %copy.201), channel_id=1, replica_groups=mesh['span'=8,'elem'=4] {'span'}, dimensions={3} | all-to-all | bytes 15925248 | tf_op jit(solution)/shard_map/all_to_all | solution.py:168
  1910.5 13.8 copy.203
  1924.3 11.3 copy.204
  (210 shorter events, 159.2 us)
Async XLA Ops:
  0.0 398.2 %copy-start = (s32[256]{0:T(256)S(1)}, s32[256]{0:T(256)}, u32[]{:S(2)}) copy-start(s32[256]{0:T(256)} %param.20) | copy-start | bytes 3076
  7.8 9.6 copy-start.2
  7.8 9.6 copy-start.3
  39.6 280.3 %all-to-all-start = ((f32[81,3,128,64]{0,3,1,2:T(8,128)}), f32[81,3,128,64]{0,3,1,2:T(8,128)}, u32[]{:S(2)}, u32[]{:S(2)}) async-start(f32[81,3,128,64]{0,3,1,2:T(8,128)} %copy.174), calls=%async_computation | async-start | bytes 25165824 | tf_op jit(solution)/shard_map/all_to_all | solution.py:95
  46.9 355.3 %copy-start.9 = (s32[512]{0:T(512)}, s32[512]{0:T(512)S(1)}, u32[]{:S(2)}) copy-start(s32[512]{0:T(512)S(1)} %mul.128) | copy-start | bytes 6148
  47.0 305.1 %copy-start.16 = (pred[512]{0:T(512)(128)(4,1)}, pred[512]{0:T(512)(128)(4,1)S(1)}, u32[]{:S(2)}) copy-start(pred[512]{0:T(512)(128)(4,1)S(1)} %eq.89) | copy-start | bytes 1540
  388.8 5.7 copy-start.6
  388.8 6.3 copy-start.20
  388.8 6.4 copy-start.15
  388.8 8.6 copy-start.19
  388.8 14.2 copy-start.18
  388.8 277.8 %all-to-all-start.1 = ((f32[81,3,16,512]{0,2,1,3:T(8,128)}), f32[81,3,16,512]{0,2,1,3:T(8,128)}, u32[]{:S(2)}, u32[]{:S(2)}) async-start(f32[81,3,16,512]{0,2,1,3:T(8,128)} %copy.177), calls=%async_computation.1 | async-start | bytes 25165824 | tf_op jit(solution)/shard_map/all_to_all | solution.py:99
  395.9 7.1 copy-start.11
  729.1 4.7 copy-start.13
  747.7 18.3 copy-start.12
  756.0 20.5 %copy-start.4 = (s32[128,4]{1,0:T(8,128)S(1)}, s32[128,4]{1,0:T(8,128)}, u32[]{:S(2)}) copy-start(s32[128,4]{1,0:T(8,128)} %get-tuple-element.410) | copy-start | bytes 6148 | tf_op jit(solution)/shard_map/while
  756.0 20.5 %copy-start.5 = (s32[128,4]{1,0:T(8,128)S(1)}, s32[128,4]{1,0:T(8,128)}, u32[]{:S(2)}) copy-start(s32[128,4]{1,0:T(8,128)} %get-tuple-element.411) | copy-start | bytes 6148 | tf_op jit(solution)/shard_map/while
  765.9 24.6 %collective-permute-start = (f32[4,9,3,64,16]{3,4,2,1,0:T(8,128)}, f32[4,9,3,64,16]{3,4,2,1,0:T(8,128)}, u32[]{:S(2)}, u32[]{:S(2)}) collective-permute-start(f32[4,9,3,64,16]{3,4,2,1,0:T(8,128)} %fusion.122), channel_id=1, source_target_pairs={{1,0},{2,1},{3,2},{0,3},{5,4},{6,5},{7,6},{4,7},{9,8},{10,9},{11,1... | collective-permute-start | bytes 1327112 | tf_op jit(solution)/shard_map/while/body/ppermute | solution.py:18
  775.9 16.3 collective-permute-start.1
  780.3 10.2 copy-start.21
  834.6 10.5 copy-start.8
  864.9 9.2 slice-start
  864.9 9.2 slice-start.1
  864.9 9.2 slice-start.2
  897.7 11.7 copy-start.7
  897.7 11.7 copy-start.14
  922.1 19.5 %copy-start.12 = (pred[128]{0:T(512)(128)(4,1)S(1)}, pred[128]{0:T(512)(128)(4,1)}, u32[]{:S(2)}) copy-start(pred[128]{0:T(512)(128)(4,1)} %get-tuple-element.414) | copy-start | bytes 388 | tf_op jit(solution)/shard_map/while
  930.5 21.5 %copy-start.4 = (s32[128,4]{1,0:T(8,128)S(1)}, s32[128,4]{1,0:T(8,128)}, u32[]{:S(2)}) copy-start(s32[128,4]{1,0:T(8,128)} %get-tuple-element.410) | copy-start | bytes 6148 | tf_op jit(solution)/shard_map/while
  930.5 21.5 %copy-start.5 = (s32[128,4]{1,0:T(8,128)S(1)}, s32[128,4]{1,0:T(8,128)}, u32[]{:S(2)}) copy-start(s32[128,4]{1,0:T(8,128)} %get-tuple-element.411) | copy-start | bytes 6148 | tf_op jit(solution)/shard_map/while
  940.4 25.6 %collective-permute-start = (f32[4,9,3,64,16]{3,4,2,1,0:T(8,128)}, f32[4,9,3,64,16]{3,4,2,1,0:T(8,128)}, u32[]{:S(2)}, u32[]{:S(2)}) collective-permute-start(f32[4,9,3,64,16]{3,4,2,1,0:T(8,128)} %fusion.122), channel_id=1, source_target_pairs={{1,0},{2,1},{3,2},{0,3},{5,4},{6,5},{7,6},{4,7},{9,8},{10,9},{11,1... | collective-permute-start | bytes 1327112 | tf_op jit(solution)/shard_map/while/body/ppermute | solution.py:18
  951.5 16.2 collective-permute-start.1
  955.8 10.2 copy-start.21
  1009.9 10.5 copy-start.8
  1040.1 9.2 slice-start
  1040.1 9.2 slice-start.1
  1040.1 9.2 slice-start.2
  1073.2 11.7 copy-start.7
  1073.2 11.7 copy-start.14
  1097.5 20.0 %copy-start.12 = (pred[128]{0:T(512)(128)(4,1)S(1)}, pred[128]{0:T(512)(128)(4,1)}, u32[]{:S(2)}) copy-start(pred[128]{0:T(512)(128)(4,1)} %get-tuple-element.414) | copy-start | bytes 388 | tf_op jit(solution)/shard_map/while
  1105.9 21.9 %copy-start.4 = (s32[128,4]{1,0:T(8,128)S(1)}, s32[128,4]{1,0:T(8,128)}, u32[]{:S(2)}) copy-start(s32[128,4]{1,0:T(8,128)} %get-tuple-element.410) | copy-start | bytes 6148 | tf_op jit(solution)/shard_map/while
  1105.9 21.9 %copy-start.5 = (s32[128,4]{1,0:T(8,128)S(1)}, s32[128,4]{1,0:T(8,128)}, u32[]{:S(2)}) copy-start(s32[128,4]{1,0:T(8,128)} %get-tuple-element.411) | copy-start | bytes 6148 | tf_op jit(solution)/shard_map/while
  1115.8 26.1 %collective-permute-start = (f32[4,9,3,64,16]{3,4,2,1,0:T(8,128)}, f32[4,9,3,64,16]{3,4,2,1,0:T(8,128)}, u32[]{:S(2)}, u32[]{:S(2)}) collective-permute-start(f32[4,9,3,64,16]{3,4,2,1,0:T(8,128)} %fusion.122), channel_id=1, source_target_pairs={{1,0},{2,1},{3,2},{0,3},{5,4},{6,5},{7,6},{4,7},{9,8},{10,9},{11,1... | collective-permute-start | bytes 1327112 | tf_op jit(solution)/shard_map/while/body/ppermute | solution.py:18
  1127.4 16.1 collective-permute-start.1
  1131.7 10.2 copy-start.21
  1185.7 10.5 copy-start.8
  1216.0 9.2 slice-start
  1216.0 9.2 slice-start.1
  1216.0 9.2 slice-start.2
  1249.0 11.7 copy-start.7
  1249.0 11.7 copy-start.14
  1281.4 5.5 copy-start.10
  1281.4 279.7 %all-to-all-start.2 = ((f32[81,3,128,64]{0,3,1,2:T(8,128)}), f32[81,3,128,64]{0,3,1,2:T(8,128)}, u32[]{:S(2)}, u32[]{:S(2)}) async-start(f32[81,3,128,64]{0,3,1,2:T(8,128)} %bitcast.305), calls=%async_computation.2 | async-start | bytes 25165824 | tf_op jit(solution)/shard_map/all_to_all | solution.py:164
  1579.6 13.9 copy-start.17
  1924.3 11.3 copy-start.1
where the time goes:
time: 1950 us; the launch traced here: 1940 us
  waiting for transfers between devices  810 us (42%)
  local copies, waits for them, and re-layouts  487 us (25%)
  blocking collectives  280 us (14%)
  matrix products  223 us (11%)
  other arithmetic  97.7 us (5%)
  starting transfers between devices  22.9 us (1%)
    all_to_all x1, blocking collectives, body(): lax.all_to_all(values, 'span', split_axis=3, concat_axis=2, tiled=True)  280 us
    all_to_all x1, waiting for transfers between devices, body(): lax.all_to_all(solution_swapped, 'span', split_axis=2, concat_axis=3, til...  274 us
    all_to_all x1, waiting for transfers between devices, body(): lax.all_to_all(source_swapped, 'span', split_axis=2, concat_axis=3, tiled...  273 us
    all_to_all x1, waiting for transfers between devices, body(): lax.all_to_all(coeffs, 'span', split_axis=3, concat_axis=2, tiled=True)  263 us
    while x78, local copies, waits for them, and re-layouts  86.6 us
    gather x6, local copies, waits for them, and re-layouts, couple(): across = gather_pool(traces)[edge_map, :, :, :, position][:, :, ::-1]  75.1 us
    rev x6, local copies, waits for them, and re-layouts, couple(): across = gather_pool(traces)[edge_map, :, :, :, position][:, :, ::-1]  51.3 us
    dot_general x4, matrix products, block_inverse(): jnp.dot(kron_basis.T, values.reshape(n_nodes, -1), precision=highest)  44.1 us
  transfers between devices with their start and end apart: 9, of which 3 were waited for; matrix products, arithmetic and copies ran while one was open for 4% of the time, Pallas kernels for 0%

commit v1 on v0

--- a/solution.py
+++ b/solution.py
@@ -1,21 +1,23 @@
+import functools
+
 import jax
 import jax.numpy as jnp
 import numpy as np
 from jax import lax
+from jax.experimental import pallas as pl
+from jax.experimental.pallas import tpu as pltpu
 from jax.sharding import PartitionSpec as P
 
 MESH_X = 16
+LANES = 128
+VMEM_BYTES = 48 * 1024 * 1024
 
 
 coupling = 0.2
 highest = lax.Precision.HIGHEST
 two_pi = 6.283185307179586
-
-
-def from_behind(block, axis, distance):
-    devices = range(lax.axis_size(axis))
-    route = [((i - distance) % len(devices), i) for i in devices]
-    return lax.ppermute(block, axis, route)
+f32 = jnp.float32
+bf16 = jnp.bfloat16
 
 
 def edge_lists(per_side):
@@ -25,6 +27,654 @@
     top_edge = [last_node * per_side + last_node - i for i in range(per_side)]
     left_edge = [(last_node - i) * per_side for i in range(per_side)]
     return [bottom, right_edge, top_edge, left_edge]
+
+
+def row_orders(n_span):
+    even = [r ^ (r >> 1 & 1) for r in range(n_span)]
+    odd = [r ^ int(2 * r >= n_span) for r in range(n_span)][::-1]
+    return [even, odd]
+
+
+def ring_route(n_span, n_elem, step):
+    orders = row_orders(n_span)
+    places = [orders[p % 2][r] * n_elem + p for p in range(n_elem) for r in range(n_span)]
+    count = len(places)
+    return [(places[g], places[(g + step) % count]) for g in range(count)]
+
+
+def split_terms(values):
+    top = values.astype(bf16)
+    return top, (values - top.astype(f32)).astype(bf16)
+
+
+def half_swap(first, second):
+    low = lax.broadcasted_iota(jnp.int32, first.shape, 1) < LANES // 2
+    left = jnp.where(low, first, pltpu.roll(second, LANES // 2, 1))
+    right = jnp.where(low, pltpu.roll(first, LANES // 2, 1), second)
+    return left, right
+
+
+def tables_kernel(n_span, n_elem, place_ref, adj_ref, map_ref, perm_ref, perm2_ref, link_ref):
+    own = adj_ref.shape[0]
+    span_id, elem_id = place_ref[0], place_ref[1]
+    lane = lax.broadcasted_iota(jnp.int32, (own, own), 1).astype(f32)
+    sub = lax.broadcasted_iota(jnp.int32, (own, own), 0).astype(f32)
+    eye = (lane == sub).astype(f32)
+    first_own = (elem_id * own).astype(f32)
+    first_next = (lax.rem(elem_id + 1, n_elem) * own).astype(f32)
+    first_prev = (lax.rem(elem_id + n_elem - 1, n_elem) * own).astype(f32)
+
+    def wide(ref, j):
+        return jnp.broadcast_to(ref[:, j : j + 1].astype(f32), (own, own))
+
+    def turned(column):
+        return jnp.sum(eye * column, axis=0, keepdims=True)
+
+    def inside(ids, first):
+        return (ids >= first) & (ids < first + own)
+
+    adj_col = [wide(adj_ref, j) for j in range(4)]
+    adj_row = [turned(c) for c in adj_col]
+    map_row = [turned(wide(map_ref, j)) for j in range(4)]
+    near = eye
+    for j in range(4):
+        near = near + (adj_col[j] - first_own == lane).astype(f32)
+    near = near.astype(bf16)
+    prev_col = jnp.zeros((own, own), f32)
+    next_col = jnp.zeros((own, own), f32)
+    for j in range(4):
+        prev_col = prev_col + jnp.where(inside(adj_col[j], first_prev), adj_col[j] + 1.0, 0.0)
+        next_col = next_col + jnp.where(inside(adj_col[j], first_next), adj_col[j] + 1.0, 0.0)
+    reached = (prev_col > 0).astype(f32)
+    row_col = 1.0 - reached
+    for _ in range(n_span - 2):
+        reached = jnp.minimum(
+            jnp.dot(near, reached.astype(bf16), preferred_element_type=f32), 1.0
+        )
+        row_col = row_col + 1.0 - reached
+    row_row = turned(row_col)
+    same = row_col == row_row
+    pos_col = jnp.sum((same & (lane < sub)).astype(f32), axis=1, keepdims=True)
+    pos_row = jnp.sum((same & (sub < lane)).astype(f32), axis=0, keepdims=True)
+    odd = lax.rem(elem_id, 2) == 1
+    orders = row_orders(n_span)
+    slot_row = jnp.zeros_like(row_row)
+    for r in range(n_span):
+        slot = jnp.where(odd, orders[1][r], orders[0][r]).astype(f32)
+        slot_row = jnp.where(row_row == float(r), slot, slot_row)
+    new_row = slot_row * float(MESH_X) + pos_row
+    perm = (sub == new_row).astype(f32).astype(bf16)
+    perm_ref[:, :own] = perm
+    perm_ref[:, own:] = perm
+    perm2_ref[:own] = perm
+    perm2_ref[own:] = perm
+
+    rank_prev = jnp.sum(
+        ((prev_col > 0) & (prev_col < turned(prev_col))).astype(f32), axis=0, keepdims=True
+    )
+    rank_next = jnp.sum(
+        ((next_col > 0) & (next_col < turned(next_col))).astype(f32), axis=0, keepdims=True
+    )
+    spot = lax.broadcasted_iota(jnp.int32, (MESH_X, own), 0).astype(f32)
+    here = new_row == spot + (span_id * MESH_X).astype(f32)
+    spot_lane = lax.broadcasted_iota(jnp.int32, (MESH_X, own), 1).astype(f32)
+    edge_up = jnp.zeros_like(row_row)
+    edge_down = jnp.zeros_like(row_row)
+
+    def chosen(values):
+        return jnp.sum(jnp.where(here, values, 0.0), axis=1, keepdims=True)
+
+    for j in range(4):
+        meets = (sub == adj_row[j] - first_own).astype(f32)
+        its_pos = jnp.sum(meets * pos_col, axis=0, keepdims=True)
+        its_row = jnp.sum(meets * row_col, axis=0, keepdims=True)
+        inner = inside(adj_row[j], first_own)
+        ahead = inside(adj_row[j], first_next)
+        behind = inside(adj_row[j], first_prev)
+        up = ahead | (inner & (its_row == row_row + 1.0))
+        down = behind | (inner & (its_row == row_row - 1.0))
+        its_pos = jnp.where(ahead, rank_next, jnp.where(behind, rank_prev, its_pos))
+        base = jnp.where(up, 4.0 * MESH_X, jnp.where(down, 5.0 * MESH_X, map_row[j] * MESH_X))
+        edge_up = jnp.where(up, float(j), edge_up)
+        edge_down = jnp.where(down, float(j), edge_down)
+        row = (spot_lane == chosen(base + its_pos)).astype(f32).astype(bf16)
+        link_ref[j * MESH_X : (j + 1) * MESH_X, :own] = row
+        link_ref[j * MESH_X : (j + 1) * MESH_X, own:] = row
+    for place, edge in ((4, edge_up), (5, edge_down)):
+        row = (spot_lane == chosen(edge * MESH_X) + spot).astype(f32).astype(bf16)
+        link_ref[place * MESH_X : (place + 1) * MESH_X, :own] = row
+        link_ref[place * MESH_X : (place + 1) * MESH_X, own:] = row
+
+
+def mesh_tables(adjacency, edge_map, n_span, n_elem):
+    own = adjacency.shape[0]
+    place = jnp.stack([lax.axis_index("span"), lax.axis_index("elem")]).astype(jnp.int32)
+    return pl.pallas_call(
+        functools.partial(tables_kernel, n_span, n_elem),
+        out_shape=(
+            jax.ShapeDtypeStruct((own, 2 * own), bf16),
+            jax.ShapeDtypeStruct((2 * own, own), bf16),
+            jax.ShapeDtypeStruct((6 * MESH_X, 2 * own), bf16),
+        ),
+        in_specs=[
+            pl.BlockSpec(memory_space=pltpu.SMEM),
+            pl.BlockSpec(memory_space=pltpu.VMEM),
+            pl.BlockSpec(memory_space=pltpu.VMEM),
+        ],
+        out_specs=[pl.BlockSpec(memory_space=pltpu.VMEM)] * 3,
+        name="mesh_tables",
+    )(place, adjacency, edge_map)
+
+
+def source_kernel(s, n_nodes, inv_ref, dref_ref, species_ref, lap_ref, perm_ref, out_ref):
+    n_species = species_ref.shape[1]
+    per_step = species_ref.shape[0]
+    zl = species_ref.shape[2]
+    n_span = out_ref.shape[0]
+    perm = perm_ref[...]
+
+    def source(n):
+        parts = [species_ref[n, j] for j in range(n_species)]
+        bath = 1.0 - sum(parts[1:], parts[0])
+        resistance = bath * inv_ref[s, n_species]
+        for j in range(n_species):
+            if j != s:
+                resistance = resistance + parts[j] * inv_ref[s, j]
+        mixture = (1.0 - parts[s]) / resistance
+        return (parts[s] + (mixture - dref_ref[s]) * lap_ref[n, 0]) / dref_ref[s]
+
+    def turned(first, second):
+        top, rest = split_terms(jnp.concatenate([first, second], axis=0))
+        both = jnp.concatenate([top, rest], axis=1)
+        return lax.dot_general(
+            perm, both, (((1,), (1,)), ((), ())), preferred_element_type=f32
+        )
+
+    def pair(k, carry):
+        tile = turned(source(2 * k), source(2 * k + 1))
+        row = pl.multiple_of(k * MESH_X, MESH_X)
+        for q in range(n_span):
+            out_ref[q, pl.ds(row, MESH_X), :] = tile[q * MESH_X : (q + 1) * MESH_X]
+        return carry
+
+    last_step = pl.num_programs(0) - 1
+
+    @pl.when(pl.program_id(0) < last_step)
+    def _():
+        lax.fori_loop(0, per_step // 2, pair, 0, unroll=2)
+
+    @pl.when(pl.program_id(0) == last_step)
+    def _():
+        value = source(0)
+        tile = turned(value, value)
+        half = MESH_X // 2
+        low = lax.broadcasted_iota(jnp.int32, (half, 2 * zl), 1) < zl
+        for q in range(n_span):
+            block = tile[q * MESH_X : (q + 1) * MESH_X]
+            out_ref[q, :half, :] = jnp.where(low, block[:half], block[half:])
+
+
+def packed_source(s, species, laplacian, inv_binary, dref, perm, n_span):
+    n_nodes, n_species, zl, own = species.shape
+    step = MESH_X
+    steps = n_nodes // step + 1
+    rows = n_nodes * MESH_X // 2
+    return pl.pallas_call(
+        functools.partial(source_kernel, s, n_nodes),
+        grid=(steps,),
+        out_shape=jax.ShapeDtypeStruct((n_span, rows, 2 * zl), f32),
+        in_specs=[
+            pl.BlockSpec(memory_space=pltpu.SMEM),
+            pl.BlockSpec(memory_space=pltpu.SMEM),
+            pl.BlockSpec((step, n_species, zl, own), lambda g: (g, 0, 0, 0)),
+            pl.BlockSpec((step, 1, zl, own), lambda g: (g, s, 0, 0)),
+            pl.BlockSpec((own, 2 * own), lambda g: (0, 0)),
+        ],
+        out_specs=pl.BlockSpec((n_span, step * MESH_X // 2, 2 * zl), lambda g: (0, g, 0)),
+        compiler_params=pltpu.CompilerParams(vmem_limit_bytes=VMEM_BYTES),
+        cost_estimate=pl.CostEstimate(
+            flops=int(species.size) * 60, bytes_accessed=int(species.size) * 7, transcendentals=0
+        ),
+        name="packed_source",
+    )(inv_binary, dref, species, laplacian, perm)
+
+
+def unpack_kernel(recv_ref, perm_ref, *refs):
+    out_ref = refs[-1]
+    n_span = recv_ref.shape[0]
+    per_step, _, zl, _ = out_ref.shape
+    perm = perm_ref[...]
+
+    def turned(tile):
+        top, rest = split_terms(tile)
+        both = jnp.concatenate([top, rest], axis=0)
+        return lax.dot_general(
+            both, perm, (((0,), (0,)), ((), ())), preferred_element_type=f32
+        )
+
+    def pair(k, carry):
+        row = pl.multiple_of(k * MESH_X, MESH_X)
+        tile = jnp.concatenate(
+            [recv_ref[q, pl.ds(row, MESH_X), :] for q in range(n_span)], axis=0
+        )
+        result = turned(tile)
+        out_ref[2 * k, 0] = result[:zl]
+        out_ref[2 * k + 1, 0] = result[zl:]
+        return carry
+
+    last_step = pl.num_programs(0) - 1
+
+    @pl.when(pl.program_id(0) < last_step)
+    def _():
+        lax.fori_loop(0, per_step // 2, pair, 0, unroll=2)
+
+    @pl.when(pl.program_id(0) == last_step)
+    def _():
+        half = MESH_X // 2
+        blocks = []
+        for q in range(n_span):
+            block = recv_ref[q, :half, :]
+            blocks += [block, pltpu.roll(block, zl, 1)]
+        out_ref[0, 0] = turned(jnp.concatenate(blocks, axis=0))[:zl]
+
+
+def unpacked(s, recv, perm2, shape, before):
+    n_nodes, n_species, zl, own = shape
+    n_span, rows, width = recv.shape
+    step = MESH_X
+    steps = n_nodes // step + 1
+    operands = [recv, perm2] + ([] if before is None else [before])
+    return pl.pallas_call(
+        unpack_kernel,
+        grid=(steps,),
+        out_shape=jax.ShapeDtypeStruct(shape, f32),
+        in_specs=[
+            pl.BlockSpec((n_span, step * MESH_X // 2, width), lambda g: (0, g, 0)),
+            pl.BlockSpec((2 * own, own), lambda g: (0, 0)),
+        ]
+        + ([] if before is None else [pl.BlockSpec(memory_space=pl.ANY)]),
+        out_specs=pl.BlockSpec((step, 1, zl, own), lambda g: (g, s, 0, 0)),
+        input_output_aliases={} if before is None else {2: 0},
+        compiler_params=pltpu.CompilerParams(vmem_limit_bytes=VMEM_BYTES),
+        cost_estimate=pl.CostEstimate(
+            flops=int(recv.size) * 512, bytes_accessed=int(recv.size) * 8, transcendentals=0
+        ),
+        name="unpacked",
+    )(*operands)
+
+
+def node_places(per_side):
+    places = {}
+    for edge, nodes in enumerate(edge_lists(per_side)):
+        for t, node in enumerate(nodes):
+            places.setdefault(node, []).append((edge, t))
+    return places
+
+
+def mix(values, weights):
+    total = values[0] * weights[0]
+    for value, weight in zip(values[1:], weights[1:]):
+        total = total + value * weight
+    return total
+
+
+def to_eigen(src, dst, basis_ref, m, cols):
+    def body(a, carry):
+        xs = [src[a * m + b, :, cols] for b in range(m)]
+        for j in range(m):
+            dst[a * m + j, :, cols] = mix(xs, [basis_ref[b, j] for b in range(m)])
+        return carry
+
+    lax.fori_loop(0, m, body, 0)
+
+
+def edges_to_eigen(field, dst, basis_ref, m, cols):
+    for a in range(m):
+        ends = range(m) if a in (0, m - 1) else (0, m - 1)
+        xs = [field(a * m + b) for b in ends]
+        for j in range(m):
+            dst[a * m + j, :, cols] = mix(xs, [basis_ref[b, j] for b in ends])
+
+
+def columns_to_eigen(src, store, basis_ref, m, cols):
+    def body(b, carry):
+        xs = [src[a * m + b, :, cols] for a in range(m)]
+        for i in range(m):
+            store(i * m + b, mix(xs, [basis_ref[a, i] for a in range(m)]))
+        return carry
+
+    lax.fori_loop(0, m, body, 0)
+
+
+def columns_from_eigen(load, dst, basis_ref, m, cols):
+    def body(b, carry):
+        xs = [load(a * m + b) for a in range(m)]
+        for i in range(m):
+            dst[i * m + b, :, cols] = mix(xs, [basis_ref[i, a] for a in range(m)])
+        return carry
+
+    lax.fori_loop(0, m, body, 0)
+
+
+def rows_from_eigen(src, store, basis_ref, m, cols):
+    def body(i, carry):
+        xs = [src[i * m + b, :, cols] for b in range(m)]
+        for j in range(m):
+            store(i * m + j, mix(xs, [basis_ref[j, b] for b in range(m)]))
+        return carry
+
+    lax.fori_loop(0, m, body, 0)
+
+
+def edge_traces(src, trace_ref, basis_ref, m, cols):
+    places = node_places(m)
+    for i in range(m):
+        xs = [src[i * m + b, :, cols] for b in range(m)]
+        for j in range(m) if i in (0, m - 1) else (0, m - 1):
+            value = mix(xs, [basis_ref[j, b] for b in range(m)])
+            for edge, t in places[i * m + j]:
+                trace_ref[t, edge * MESH_X : (edge + 1) * MESH_X, cols] = value
+
+
+def picked(link, blocks):
+    pad = link.shape[1] // 2 - sum(block.shape[0] for block in blocks)
+    blocks = blocks + [jnp.zeros((pad, blocks[0].shape[1]), f32)]
+    top, rest = split_terms(jnp.concatenate(blocks, axis=0))
+    return jnp.dot(link, jnp.concatenate([top, rest], axis=0), preferred_element_type=f32)
+
+
+def send_traces(trace_ref, link_ref, up_ref, down_ref, m):
+    link = link_ref[4 * MESH_X : 6 * MESH_X, :]
+    for t in range(m):
+        out = picked(link, [trace_ref[t]])
+        up_ref[t] = out[:MESH_X]
+        down_ref[t] = out[MESH_X:]
+
+
+def column_blocks(width, block):
+    return [slice(c, c + block) for c in range(0, width, block)]
+
+
+BLOCK = 256
+
+
+def start_kernel(
+    m, basis_ref, recv_ref, top_ref, rest_ref, diag_ref, link_ref,
+    w_ref, trace_ref, up_ref, down_ref, xt, xr, y,
+):
+    n_span, rows, width = recv_ref.shape
+    n_nodes = m * m
+    planes = top_ref.shape[0]
+
+    def place(node, first, second, tile):
+        lanes = slice(tile * LANES, (tile + 1) * LANES)
+        for offset, value in ((0, first), (1, second)):
+            top, rest = split_terms(value)
+            row = pl.multiple_of((node + offset) * MESH_X, MESH_X)
+            xt[pl.ds(row, MESH_X), lanes] = top
+            xr[pl.ds(row, MESH_X), lanes] = rest
+
+    def pair(k, carry):
+        row = pl.multiple_of(k * MESH_X, MESH_X)
+        for tile in range(n_span // 2):
+            left, right = half_swap(
+                recv_ref[2 * tile, pl.ds(row, MESH_X), :],
+                recv_ref[2 * tile + 1, pl.ds(row, MESH_X), :],
+            )
+            place(2 * k, left, right, tile)
+        return carry
+
+    lax.fori_loop(0, n_nodes // 2, pair, 0)
+    half = MESH_X // 2
+    last = n_nodes // 2 * MESH_X
+    for tile in range(n_span // 2):
+        left, right = half_swap(
+            recv_ref[2 * tile, last : last + half, :],
+            recv_ref[2 * tile + 1, last : last + half, :],
+        )
+        lanes = slice(tile * LANES, (tile + 1) * LANES)
+        top, rest = split_terms(jnp.concatenate([left, right], axis=0))
+        xt[2 * last :, lanes] = top
+        xr[2 * last :, lanes] = rest
+
+    chunk = m * MESH_X
+
+    def transform(c, carry):
+        rows_c = pl.ds(pl.multiple_of(c * chunk, chunk), chunk)
+        top, rest = xt[rows_c, :], xr[rows_c, :]
+        out = jnp.dot(top, top_ref[...], preferred_element_type=f32)
+        out = out + jnp.dot(rest, top_ref[...], preferred_element_type=f32)
+        out = out + jnp.dot(top, rest_ref[...], preferred_element_type=f32)
+        y[pl.ds(c * m, m)] = out.reshape(m, MESH_X, planes)
+        return carry
+
+    lax.fori_loop(0, m, transform, 0)
+
+    for cols in column_blocks(planes, BLOCK):
+        to_eigen(y, y, basis_ref, m, cols)
+
+        def store(n, value, cols=cols):
+            w_ref[n, :, cols] = value
+
+        columns_to_eigen(y, store, basis_ref, m, cols)
+
+        def load(n, cols=cols):
+            return w_ref[n, :, cols] * diag_ref[n, :, cols]
+
+        columns_from_eigen(load, y, basis_ref, m, cols)
+        edge_traces(y, trace_ref, basis_ref, m, cols)
+    send_traces(trace_ref, link_ref, up_ref, down_ref, m)
+
+
+def coupled_values(m, trace_ref, above_ref, below_ref, link_ref, g):
+    link = link_ref[: 4 * MESH_X, :]
+    for t in range(m):
+        back = m - 1 - t
+        g[t] = picked(link, [trace_ref[back], above_ref[back], below_ref[back]])
+
+
+def sweep_values(m, sweep_id, basis_ref, rounds_ref, w_ref, v_ref, diag_ref, g, y, vout, cols):
+    places = node_places(m)
+
+    def field(node):
+        total = None
+        for edge, t in places[node]:
+            value = g[t, edge * MESH_X : (edge + 1) * MESH_X, cols]
+            total = value if total is None else total + value
+        return total * coupling
+
+    edges_to_eigen(field, y, basis_ref, m, cols)
+    going = rounds_ref[:, cols] > sweep_id
+
+    def store(n, value):
+        vout[n, :, cols] = jnp.where(going, w_ref[n, :, cols] + value, v_ref[n, :, cols])
+
+    columns_to_eigen(y, store, basis_ref, m, cols)
+
+    def load(n):
+        return vout[n, :, cols] * diag_ref[n, :, cols]
+
+    columns_from_eigen(load, y, basis_ref, m, cols)
+
+
+def sweep_kernel(
+    m, sweep_id, basis_ref, rounds_ref, w_ref, v_ref, diag_ref, link_ref, trace_ref, above_ref,
+    below_ref, vout_ref, tout_ref, up_ref, down_ref, g, y,
+):
+    width = w_ref.shape[2]
+    coupled_values(m, trace_ref, above_ref, below_ref, link_ref, g)
+    for cols in column_blocks(width, min(BLOCK, width)):
+        sweep_values(
+            m, sweep_id, basis_ref, rounds_ref, w_ref, v_ref, diag_ref, g, y, vout_ref, cols
+        )
+        edge_traces(y, tout_ref, basis_ref, m, cols)
+    send_traces(tout_ref, link_ref, up_ref, down_ref, m)
+
+
+def finish_kernel(
+    m, sweep_id, basis_ref, rounds_ref, w_ref, v_ref, diag_ref, link_ref, trace_ref, above_ref,
+    below_ref, top_ref, rest_ref, out_ref, g, y, vout, mt, mr,
+):
+    n_nodes = m * m
+    n_span = out_ref.shape[0]
+    planes = top_ref.shape[0]
+    coupled_values(m, trace_ref, above_ref, below_ref, link_ref, g)
+    for cols in column_blocks(planes, BLOCK):
+        sweep_values(m, sweep_id, basis_ref, rounds_ref, w_ref, v_ref, diag_ref, g, y, vout, cols)
+
+        def store(n, value, cols=cols):
+            row = pl.multiple_of(n * MESH_X, MESH_X)
+            top, rest = split_terms(value)
+            mt[pl.ds(row, MESH_X), cols] = top
+            mr[pl.ds(row, MESH_X), cols] = rest
+
+        rows_from_eigen(y, store, basis_ref, m, cols)
+
+    chunk = m * MESH_X
+
+    def transform(c, carry):
+        rows_c = pl.ds(pl.multiple_of(c * chunk, chunk), chunk)
+        top, rest = mt[rows_c, :], mr[rows_c, :]
+        out = jnp.dot(top, top_ref[...], preferred_element_type=f32)
+        out = out + jnp.dot(rest, top_ref[...], preferred_element_type=f32)
+        out = out + jnp.dot(top, rest_ref[...], preferred_element_type=f32)
+        y[pl.ds(c * m, m)] = out.reshape(m, MESH_X, planes)
+        return carry
+
+    lax.fori_loop(0, m, transform, 0)
+
+    def pair(k, carry):
+        row = pl.multiple_of(k * MESH_X, MESH_X)
+        for tile in range(n_span // 2):
+            lanes = slice(tile * LANES, (tile + 1) * LANES)
+            left, right = half_swap(y[2 * k, :, lanes], y[2 * k + 1, :, lanes])
+            out_ref[2 * tile, pl.ds(row, MESH_X), :] = left
+            out_ref[2 * tile + 1, pl.ds(row, MESH_X), :] = right
+        return carry
+
+    lax.fori_loop(0, n_nodes // 2, pair, 0)
+    half = MESH_X // 2
+    last = n_nodes // 2 * MESH_X
+    for tile in range(n_span // 2):
+        lanes = slice(tile * LANES, (tile + 1) * LANES)
+        left, right = half_swap(y[n_nodes - 1, :half, lanes], y[n_nodes - 1, half:, lanes])
+        out_ref[2 * tile, last : last + half, :] = left
+        out_ref[2 * tile + 1, last : last + half, :] = right
+
+
+def vmem_call(kernel, name, out_shape, scratch, flops, operands):
+    bytes_moved = sum(int(x.size) * x.dtype.itemsize for x in list(operands) + list(out_shape))
+    smem = pl.BlockSpec(memory_space=pltpu.SMEM)
+    vmem = pl.BlockSpec(memory_space=pltpu.VMEM)
+    return pl.pallas_call(
+        kernel,
+        out_shape=tuple(out_shape),
+        in_specs=[smem] + [vmem] * (len(operands) - 1),
+        out_specs=tuple([vmem] * len(out_shape)),
+        scratch_shapes=scratch,
+        compiler_params=pltpu.CompilerParams(vmem_limit_bytes=VMEM_BYTES),
+        cost_estimate=pl.CostEstimate(
+            flops=flops, bytes_accessed=bytes_moved, transcendentals=0
+        ),
+        name=name,
+    )(*operands)
+
+
+def solve_species(recv, basis, rounds_row, diag, link, forward, backward, n_span, n_elem):
+    m = basis.shape[0]
+    n_nodes = m * m
+    planes = forward[0].shape[0]
+    field = jax.ShapeDtypeStruct((n_nodes, MESH_X, planes), f32)
+    trace = jax.ShapeDtypeStruct((m, 4 * MESH_X, planes), f32)
+    side = jax.ShapeDtypeStruct((m, MESH_X, planes), f32)
+    terms = pltpu.VMEM((n_nodes * MESH_X, planes), bf16)
+    work = pltpu.VMEM(field.shape, f32)
+    gathered = pltpu.VMEM(trace.shape, f32)
+    transform_flops = 6 * n_nodes * MESH_X * planes * planes
+    mix_flops = 600 * n_nodes * MESH_X * planes
+    axes = ("span", "elem")
+    to_next = ring_route(n_span, n_elem, 1)
+    to_prev = ring_route(n_span, n_elem, -1)
+
+    def exchange(up, down):
+        below = lax.ppermute(up, axes, to_next)
+        above = lax.ppermute(down, axes, to_prev)
+        return above, below
+
+    w, traces, up, down = vmem_call(
+        functools.partial(start_kernel, m),
+        "start_solve",
+        [field, trace, side, side],
+        [terms, terms, work],
+        transform_flops + mix_flops,
+        [basis, recv, forward[0], forward[1], diag, link],
+    )
+    v = w
+    for sweep_id in (1, 2):
+        above, below = exchange(up, down)
+        v, traces, up, down = vmem_call(
+            functools.partial(sweep_kernel, m, sweep_id),
+            "sweep_solve",
+            [field, trace, side, side],
+            [gathered, work],
+            mix_flops,
+            [basis, rounds_row, w, v, diag, link, traces, above, below],
+        )
+    above, below = exchange(up, down)
+    (result,) = vmem_call(
+        functools.partial(finish_kernel, m, 3),
+        "finish_solve",
+        [jax.ShapeDtypeStruct(recv.shape, f32)],
+        [gathered, work, work, terms, terms],
+        transform_flops + mix_flops,
+        [basis, rounds_row, w, v, diag, link, traces, above, below, backward[0], backward[1]],
+    )
+    return result
+
+
+def outer_split(values):
+    top = lax.reduce_precision(values, exponent_bits=8, mantissa_bits=7)
+    return top.astype(bf16), (values - top).astype(bf16)
+
+
+def row_body(species, laplacian, binary, dref, stiff_eig, basis, rounds, adjacency, edge_map):
+    n_nodes, n_species, zl, own = species.shape
+    n_span = lax.axis_size("span")
+    n_elem = lax.axis_size("elem")
+    planes = zl * n_span
+    n_modes = planes // 2
+    perm, perm2, link = mesh_tables(adjacency, edge_map, n_span, n_elem)
+    inv_binary = 1.0 / binary
+    arrived = []
+    for s in range(n_species):
+        sent = packed_source(s, species, laplacian, inv_binary, dref, perm, n_span)
+        arrived.append(lax.all_to_all(sent, "span", split_axis=0, concat_axis=0, tiled=True))
+
+    col_mode = jnp.tile(jnp.arange(n_modes, dtype=jnp.int32), 2)
+    col_part = jnp.repeat(jnp.arange(2, dtype=jnp.int32), n_modes)
+    table_in, table_out = transform_tables(col_mode, col_part, planes)
+    forward = outer_split(table_in)
+    backward = outer_split(table_out)
+    wavenumber = col_mode.astype(f32) * (8.0 / planes)
+    shifts = 1.0 / dref[:, None] + (wavenumber * wavenumber)[None, :]
+    eig_sum = (stiff_eig[:, None] + stiff_eig[None, :]).reshape(n_nodes)
+    diag = 1.0 / (shifts[:, None, None, :] + eig_sum[None, :, None, None])
+    rounds_row = jnp.tile(rounds, 2).reshape(1, planes)
+
+    updated = None
+    for s in range(n_species):
+        result = solve_species(
+            arrived[s], basis, rounds_row, diag[s], link, forward, backward, n_span, n_elem
+        )
+        back = lax.all_to_all(result, "span", split_axis=0, concat_axis=0, tiled=True)
+        updated = unpacked(s, back, perm2, species.shape, updated)
+    return updated
+
+
+def from_behind(block, axis, distance):
+    devices = range(lax.axis_size(axis))
+    route = [((i - distance) % len(devices), i) for i in devices]
+    return lax.ppermute(block, axis, route)
 
 
 def edge_matrix(per_side):
@@ -170,8 +820,15 @@
 
 
 def solution(mesh):
+    n_span, n_elem = mesh.shape["span"], mesh.shape["elem"]
+
+    def chosen_body(species, *rest):
+        zl, own = species.shape[2:]
+        by_rows = n_span * MESH_X == own and 2 * zl == LANES == own and n_elem > 2
+        return (row_body if by_rows else body)(species, *rest)
+
     return jax.shard_map(
-        body,
+        chosen_body,
         mesh=mesh,
         in_specs=(
             P(None, None, "span", "elem"),

time: 1950 us -> 610 us (0.31)
  waiting for transfers between devices: 810 us -> 267 us
  local copies, waits for them, and re-layouts: 487 us -> 22.6 us
  blocking collectives: 280 us -> 0 us
  matrix products: 223 us -> 0 us
  Pallas kernels: 0 us -> 209 us
  other arithmetic: 97.7 us -> 11.3 us
  starting transfers between devices: 22.9 us -> 89.8 us
    all_to_all x3 -> x6, waiting for transfers between devices: 810 us -> 148 us  [the longest x3 102 us: row_body(): lax.all_to_all(sent, 'span', split_axis=0, concat_axis=0, tiled=True)]
    all_to_all x1 -> x0, blocking collectives: 280 us -> none  [body(): lax.all_to_all(values, 'span', split_axis=3, concat_axis=2, tiled=True)]
    dot_general x19 -> x0, matrix products: 223 us -> none  [the longest x4 44.1 us: block_inverse(): jnp.dot(kron_basis.T, values.reshape(n_nodes, -1), precision=highest)]
    pallas_call x0 -> x19, Pallas kernels: none -> 209 us  [the longest x12 158 us: vmem_call(): pl.pallas_call(kernel, out_shape=tuple(out_shape), in_specs=[smem] + [vme...]
    ppermute x6 -> x18, waiting for transfers between devices: 0.02 us -> 119 us  [the longest x9 85.7 us: exchange(): above = lax.ppermute(down, axes, to_prev)]
    gather x14 -> x0, local copies, waits for them, and re-layouts: 114 us -> none  [the longest x6 75.1 us: couple(): across = gather_pool(traces)[edge_map, :, :, :, position][:, :, ::-1]]
    while x79 -> x0, local copies, waits for them, and re-layouts: 97.7 us -> none
    all_to_all x6 -> x0, local copies, waits for them, and re-layouts: 92.3 us -> none  [the longest x2 32.3 us: body(): lax.all_to_all(source_swapped, 'span', split_axis=2, concat_axis=3, tiled...]
  transfers between devices with their start and end apart: 9 -> 24, of which waited for: 3 -> 15; matrix products, arithmetic and copies ran while one was open for 4% -> 2% of each run, Pallas kernels for 0% -> 32%
where the time goes in v1:
time: 610 us; the launch traced here: 600 us
  waiting for transfers between devices  267 us (44%)
  Pallas kernels  209 us (34%)
  starting transfers between devices  89.8 us (15%)
  local copies, waits for them, and re-layouts  22.6 us (4%)
  other arithmetic  11.3 us (2%)
    pallas_call x12, Pallas kernels, vmem_call(): pl.pallas_call(kernel, out_shape=tuple(out_shape), in_specs=[smem] + [vme...  158 us
    all_to_all x3, waiting for transfers between devices, row_body(): lax.all_to_all(sent, 'span', split_axis=0, concat_axis=0, tiled=True)  102 us
    ppermute x9, waiting for transfers between devices, exchange(): above = lax.ppermute(down, axes, to_prev)  85.7 us
    all_to_all x3, waiting for transfers between devices, row_body(): lax.all_to_all(result, 'span', split_axis=0, concat_axis=0, tiled=True)  46.4 us
    all_to_all x3, starting transfers between devices, row_body(): lax.all_to_all(result, 'span', split_axis=0, concat_axis=0, tiled=True)  33.1 us
    ppermute x9, waiting for transfers between devices, exchange(): below = lax.ppermute(up, axes, to_next)  33 us
    ppermute x9, starting transfers between devices, exchange(): below = lax.ppermute(up, axes, to_next)  28.4 us
    pallas_call x3, Pallas kernels, packed_source(): pl.pallas_call(functools.partial(source_kernel, s, n_nodes), grid=(steps,...  26.6 us
  transfers between devices with their start and end apart: 24, of which 15 were waited for; matrix products, arithmetic and copies ran while one was open for 2% of the time, Pallas kernels for 32%

profile of v1, /device:TPU:0, one launch (start us, length us, event | category | flops | bytes accessed | tf_op | source)
XLA Modules:
  0.0 600.2 jit_solution(13462284388864372479)
XLA Ops:
  0.7 1.4 copy.12.adj_ref
  2.1 1.4 copy.13.map_ref
  4.1 2.7 mesh_tables.1
  8.3 8.8 %packed_source.3 = f32[8,648,128]{2,1,0:T(8,128)} custom-call(f32[3,4]{1,0:T(4,128)S(1)} %broadcast_divide_fusion.inv_ref, f32[3]{0:T(128)S(1)} %copy-done.23, f32[81,3,64,128]{3,2,1,0:T(8,128)} %species_ref.5, f32[81,3,64,128]{3,2,1,0:T(8,128)} %lap_ref.5, bf16[128,256]{1,0:T(8,128)(2,1)S(1)} %copy-done.15), custom_call_target="tpu_custom_call" | custom-call | flops 119439360 | bytes 13934592 | tf_op jit(solution)/shard_map/packed_source/pallas_call | solution.py:222
  17.2 7.4 %all-to-all-start = ((f32[8,648,128]{2,1,0:T(8,128)}), f32[8,648,128]{2,1,0:T(8,128)S(1)}, u32[]{:S(2)}, u32[]{:S(2)}) async-start(f32[8,648,128]{2,1,0:T(8,128)} %packed_source.3), calls=%async_computation | async-start | bytes 5308416 | tf_op jit(solution)/shard_map/all_to_all | solution.py:651
  24.6 8.9 %packed_source.4 = f32[8,648,128]{2,1,0:T(8,128)} custom-call(f32[3,4]{1,0:T(4,128)S(1)} %broadcast_divide_fusion.inv_ref, f32[3]{0:T(128)S(1)} %copy-done.24, f32[81,3,64,128]{3,2,1,0:T(8,128)} %species_ref.5, f32[81,3,64,128]{3,2,1,0:T(8,128)} %lap_ref.5, bf16[128,256]{1,0:T(8,128)(2,1)S(1)} %copy-done.16), custom_call_target="tpu_custom_call" | custom-call | flops 119439360 | bytes 13934592 | tf_op jit(solution)/shard_map/packed_source/pallas_call | solution.py:222
  33.5 51.2 %all-to-all-done.recv_ref = f32[8,648,128]{2,1,0:T(8,128)S(1)} async-done(((f32[8,648,128]{2,1,0:T(8,128)}), f32[8,648,128]{2,1,0:T(8,128)S(1)}, u32[]{:S(2)}, u32[]{:S(2)}) %all-to-all-start) | async-done | bytes 2654240 | tf_op jit(solution)/shard_map/all_to_all | solution.py:651
  84.7 1.5 copy-done.25
  86.2 4.4 all-to-all-start.2
  90.7 8.9 %packed_source.5 = f32[8,648,128]{2,1,0:T(8,128)} custom-call(f32[3,4]{1,0:T(4,128)S(1)} %broadcast_divide_fusion.inv_ref, f32[3]{0:T(128)S(1)} %copy-done.24, f32[81,3,64,128]{3,2,1,0:T(8,128)} %species_ref.5, f32[81,3,64,128]{3,2,1,0:T(8,128)} %lap_ref.5, bf16[128,256]{1,0:T(8,128)(2,1)S(1)} %copy-done.16), custom_call_target="tpu_custom_call" | custom-call | flops 119439360 | bytes 13934592 | tf_op jit(solution)/shard_map/packed_source/pallas_call | solution.py:222
  99.6 50.8 %all-to-all-done.2.recv_ref = f32[8,648,128]{2,1,0:T(8,128)} async-done(((f32[8,648,128]{2,1,0:T(8,128)}), f32[8,648,128]{2,1,0:T(8,128)}, u32[]{:S(2)}, u32[]{:S(2)}) %all-to-all-start.2) | async-done | bytes 2654240 | tf_op jit(solution)/shard_map/all_to_all | solution.py:651
  150.3 3.6 all-to-all-start.4
  155.9 9.3 %fusion.1 = (bf16[512,512]{1,0:T(8,128)(2,1)S(1)}, bf16[512,512]{1,0:T(8,128)(2,1)S(1)}, bf16[512,512]{1,0:T(8,128)(2,1)S(1)}, bf16[512,512]{1,0:T(8,128)(2,1)S(1)}) fusion(f32[512]{0:T(512)S(1)} %get-tuple-element.90, s32[512]{0:T(512)S(1)} %bitcast.25, pred[512]{0:T(512)(128)(4,1)S(1)} %eq.82), kind=kLoop, calls=%fused_computation.11 | loop fusion | flops 11010048 | bytes 2101760 | tf_op jit(solution)/shard_map/convert_element_type | solution.py:637
  165.3 16.0 %start_solve.4 = (f32[81,16,512]{2,1,0:T(8,128)S(1)}, f32[9,64,512]{2,1,0:T(8,128)S(1)}, f32[9,16,512]{2,1,0:T(8,128)S(1)}, f32[9,16,512]{2,1,0:T(8,128)S(1)}) custom-call(f32[9,9]{1,0:T(8,128)S(1)} %copy-done.13, f32[8,648,128]{2,1,0:T(8,128)} %all-to-all-done.2.recv_ref, bf16[512,512]{1,0:T(8,128)(2,1)S(1)} %get-tuple-element.89.top_ref, ...), custom_call_target="tpu_custom_call" | custom-call | flops 2436562944 | bytes 8341828 | tf_op jit(solution)/shard_map/start_solve/pallas_call | solution.py:569
  181.3 1.5 copy-done.3
  183.7 1.2 collective-permute-start.7
  184.9 14.8 %collective-permute-done.6.above_ref = f32[9,16,512]{2,1,0:T(8,128)S(1)} collective-permute-done((f32[9,16,512]{2,1,0:T(8,128)S(1)}, f32[9,16,512]{2,1,0:T(8,128)S(1)}, u32[]{:S(2)}, u32[]{:S(2)}) %collective-permute-start.6) | collective-permute-done | bytes 294944 | tf_op jit(solution)/shard_map/ppermute | solution.py:601
  199.6 10.1 %sweep_solve.8 = (f32[81,16,512]{2,1,0:T(8,128)}, f32[9,64,512]{2,1,0:T(8,128)S(1)}, f32[9,16,512]{2,1,0:T(8,128)S(1)}, f32[9,16,512]{2,1,0:T(8,128)S(1)}) custom-call(f32[9,9]{1,0:T(8,128)S(1)} %copy-done.13, s32[1,512]{1,0:T(1,128)S(1)} %bitcast.15, f32[81,16,512]{2,1,0:T(8,128)} %copy-done.3, f32[81,16,512]{2,1,0:T(8,128)} %copy-done.3, ...), custom_call_target="tpu_custom_call" | custom-call | flops 398131200 | bytes 11718980 | tf_op jit(solution)/shard_map/sweep_solve/pallas_call | solution.py:569
  209.7 1.2 collective-permute-start.8
  210.9 5.0 collective-permute-start.9
  216.0 5.7 collective-permute-done.8.above_ref
  221.7 10.1 %sweep_solve.9 = (f32[81,16,512]{2,1,0:T(8,128)}, f32[9,64,512]{2,1,0:T(8,128)S(1)}, f32[9,16,512]{2,1,0:T(8,128)S(1)}, f32[9,16,512]{2,1,0:T(8,128)S(1)}) custom-call(f32[9,9]{1,0:T(8,128)S(1)} %copy-done.13, s32[1,512]{1,0:T(1,128)S(1)} %bitcast.16, f32[81,16,512]{2,1,0:T(8,128)} %copy-done.3, f32[81,16,512]{2,1,0:T(8,128)} %get-tuple-element.63.v_ref, ...), custom_call_target="tpu_custom_call" | custom-call | flops 398131200 | bytes 11718980 | tf_op jit(solution)/shard_map/sweep_solve/pallas_call | solution.py:569
  231.8 2.9 collective-permute-start.10
  235.1 4.7 collective-permute-done.10.above_ref
  239.8 11.4 %collective-permute-done.11.below_ref = f32[9,16,512]{2,1,0:T(8,128)S(1)} collective-permute-done((f32[9,16,512]{2,1,0:T(8,128)S(1)}, f32[9,16,512]{2,1,0:T(8,128)S(1)}, u32[]{:S(2)}, u32[]{:S(2)}) %collective-permute-start.11) | collective-permute-done | bytes 294944 | tf_op jit(solution)/shard_map/ppermute | solution.py:600
  251.2 17.0 %finish_solve.4 = f32[8,648,128]{2,1,0:T(8,128)S(1)} custom-call(f32[9,9]{1,0:T(8,128)S(1)} %copy-done.13, s32[1,512]{1,0:T(1,128)S(1)} %bitcast.17, f32[81,16,512]{2,1,0:T(8,128)} %copy-done.3, f32[81,16,512]{2,1,0:T(8,128)} %get-tuple-element.67.v_ref, f32[81,1,512]{2,1,0:T(1,128)S(1)} %get-tuple-element.84.diag_ref, bf16[96,256]{1,0:T(8,128)(2,1)S(1)} %copy-done.11, ...), custom_call_target="tpu_custom_call" | custom-call | flops 2436562944 | bytes 10998084 | tf_op jit(solution)/shard_map/finish_solve/pallas_call | solution.py:569
  268.2 1.5 copy-done.6
  269.7 1.5 copy-done.26
  271.2 10.7 %all-to-all-start.3 = ((f32[8,648,128]{2,1,0:T(8,128)}), f32[8,648,128]{2,1,0:T(8,128)S(1)}, u32[]{:S(2)}, u32[]{:S(2)}) async-start(f32[8,648,128]{2,1,0:T(8,128)} %copy-done.6), calls=%async_computation.3 | async-start | bytes 5308416 | tf_op jit(solution)/shard_map/all_to_all | solution.py:669
  282.8 1.0 copy-done.18
  284.9 15.5 %start_solve.5 = (f32[81,16,512]{2,1,0:T(8,128)S(1)}, f32[9,64,512]{2,1,0:T(8,128)S(1)}, f32[9,16,512]{2,1,0:T(8,128)S(1)}, f32[9,16,512]{2,1,0:T(8,128)S(1)}) custom-call(f32[9,9]{1,0:T(8,128)S(1)} %copy-done.13, f32[8,648,128]{2,1,0:T(8,128)} %copy-done.26, bf16[512,512]{1,0:T(8,128)(2,1)S(1)} %copy-done.21, bf16[512,512]{1,0:T(8,128)(2,1)S(1)} %copy-done.18, ...), custom_call_target="tpu_custom_call" | custom-call | flops 2436562944 | bytes 8341828 | tf_op jit(solution)/shard_map/start_solve/pallas_call | solution.py:569
  300.4 1.5 copy-done.4
  302.0 2.0 collective-permute-start.13
  303.9 20.0 %collective-permute-done.12.above_ref = f32[9,16,512]{2,1,0:T(8,128)S(1)} collective-permute-done((f32[9,16,512]{2,1,0:T(8,128)S(1)}, f32[9,16,512]{2,1,0:T(8,128)S(1)}, u32[]{:S(2)}, u32[]{:S(2)}) %collective-permute-start.12) | collective-permute-done | bytes 294944 | tf_op jit(solution)/shard_map/ppermute | solution.py:601
  323.9 10.1 %sweep_solve.10 = (f32[81,16,512]{2,1,0:T(8,128)}, f32[9,64,512]{2,1,0:T(8,128)S(1)}, f32[9,16,512]{2,1,0:T(8,128)S(1)}, f32[9,16,512]{2,1,0:T(8,128)S(1)}) custom-call(f32[9,9]{1,0:T(8,128)S(1)} %copy-done.13, s32[1,512]{1,0:T(1,128)S(1)} %bitcast.18, f32[81,16,512]{2,1,0:T(8,128)} %copy-done.4, f32[81,16,512]{2,1,0:T(8,128)} %copy-done.4, ...), custom_call_target="tpu_custom_call" | custom-call | flops 398131200 | bytes 11718980 | tf_op jit(solution)/shard_map/sweep_solve/pallas_call | solution.py:569
  334.0 1.2 collective-permute-start.14
  335.2 7.8 %collective-permute-start.15 = (f32[9,16,512]{2,1,0:T(8,128)S(1)}, f32[9,16,512]{2,1,0:T(8,128)S(1)}, u32[]{:S(2)}, u32[]{:S(2)}) collective-permute-start(f32[9,16,512]{2,1,0:T(8,128)S(1)} %get-tuple-element.78), channel_id=1, source_target_pairs={{0,4},{4,12},{12,8},{8,16},{16,20},{20,28},{28,24},{24,25},{25,29}... | collective-permute-start | bytes 884744 | tf_op jit(solution)/shard_map/ppermute | solution.py:600
  343.0 7.0 %collective-permute-done.14.above_ref = f32[9,16,512]{2,1,0:T(8,128)S(1)} collective-permute-done((f32[9,16,512]{2,1,0:T(8,128)S(1)}, f32[9,16,512]{2,1,0:T(8,128)S(1)}, u32[]{:S(2)}, u32[]{:S(2)}) %collective-permute-start.14) | collective-permute-done | bytes 294944 | tf_op jit(solution)/shard_map/ppermute | solution.py:601
  350.0 10.2 %sweep_solve.11 = (f32[81,16,512]{2,1,0:T(8,128)}, f32[9,64,512]{2,1,0:T(8,128)S(1)}, f32[9,16,512]{2,1,0:T(8,128)S(1)}, f32[9,16,512]{2,1,0:T(8,128)S(1)}) custom-call(f32[9,9]{1,0:T(8,128)S(1)} %copy-done.13, s32[1,512]{1,0:T(1,128)S(1)} %bitcast.19, f32[81,16,512]{2,1,0:T(8,128)} %copy-done.4, f32[81,16,512]{2,1,0:T(8,128)} %get-tuple-element.75.v_ref, ...), custom_call_target="tpu_custom_call" | custom-call | flops 398131200 | bytes 11718980 | tf_op jit(solution)/shard_map/sweep_solve/pallas_call | solution.py:569
  360.2 1.6 collective-permute-start.16
  362.2 4.7 collective-permute-done.16.above_ref
  366.9 10.6 %collective-permute-done.17.below_ref = f32[9,16,512]{2,1,0:T(8,128)S(1)} collective-permute-done((f32[9,16,512]{2,1,0:T(8,128)S(1)}, f32[9,16,512]{2,1,0:T(8,128)S(1)}, u32[]{:S(2)}, u32[]{:S(2)}) %collective-permute-start.17) | collective-permute-done | bytes 294944 | tf_op jit(solution)/shard_map/ppermute | solution.py:600
  377.5 16.9 %finish_solve.5 = f32[8,648,128]{2,1,0:T(8,128)S(1)} custom-call(f32[9,9]{1,0:T(8,128)S(1)} %copy-done.13, s32[1,512]{1,0:T(1,128)S(1)} %bitcast.20, f32[81,16,512]{2,1,0:T(8,128)} %copy-done.4, f32[81,16,512]{2,1,0:T(8,128)} %get-tuple-element.79.v_ref, f32[81,1,512]{2,1,0:T(1,128)S(1)} %copy-done.12, bf16[96,256]{1,0:T(8,128)(2,1)S(1)} %copy-done.11, ...), custom_call_target="tpu_custom_call" | custom-call | flops 2436562944 | bytes 10998084 | tf_op jit(solution)/shard_map/finish_solve/pallas_call | solution.py:569
  394.4 1.6 copy-done.5
  396.0 11.2 %all-to-all-start.5 = ((f32[8,648,128]{2,1,0:T(8,128)}), f32[8,648,128]{2,1,0:T(8,128)}, u32[]{:S(2)}, u32[]{:S(2)}) async-start(f32[8,648,128]{2,1,0:T(8,128)} %copy-done.5), calls=%async_computation.5 | async-start | bytes 5308416 | tf_op jit(solution)/shard_map/all_to_all | solution.py:669
  409.3 15.4 %start_solve.3 = (f32[81,16,512]{2,1,0:T(8,128)S(1)}, f32[9,64,512]{2,1,0:T(8,128)S(1)}, f32[9,16,512]{2,1,0:T(8,128)S(1)}, f32[9,16,512]{2,1,0:T(8,128)S(1)}) custom-call(f32[9,9]{1,0:T(8,128)S(1)} %copy-done.13, f32[8,648,128]{2,1,0:T(8,128)} %copy-done.25, bf16[512,512]{1,0:T(8,128)(2,1)S(1)} %copy-done.22, bf16[512,512]{1,0:T(8,128)(2,1)S(1)} %copy-done.19, ...), custom_call_target="tpu_custom_call" | custom-call | flops 2436562944 | bytes 8341828 | tf_op jit(solution)/shard_map/start_solve/pallas_call | solution.py:569
  424.8 1.5 copy-done.2
  426.4 1.9 collective-permute-start.1
  428.3 17.5 %collective-permute-done.above_ref = f32[9,16,512]{2,1,0:T(8,128)S(1)} collective-permute-done((f32[9,16,512]{2,1,0:T(8,128)S(1)}, f32[9,16,512]{2,1,0:T(8,128)S(1)}, u32[]{:S(2)}, u32[]{:S(2)}) %collective-permute-start) | collective-permute-done | bytes 294944 | tf_op jit(solution)/shard_map/ppermute | solution.py:601
  445.8 10.1 %sweep_solve.6 = (f32[81,16,512]{2,1,0:T(8,128)}, f32[9,64,512]{2,1,0:T(8,128)S(1)}, f32[9,16,512]{2,1,0:T(8,128)S(1)}, f32[9,16,512]{2,1,0:T(8,128)S(1)}) custom-call(f32[9,9]{1,0:T(8,128)S(1)} %copy-done.13, s32[1,512]{1,0:T(1,128)S(1)} %bitcast.21, f32[81,16,512]{2,1,0:T(8,128)} %copy-done.2, f32[81,16,512]{2,1,0:T(8,128)} %copy-done.2, ...), custom_call_target="tpu_custom_call" | custom-call | flops 398131200 | bytes 11718980 | tf_op jit(solution)/shard_map/sweep_solve/pallas_call | solution.py:569
  455.9 3.0 collective-permute-start.2
  458.8 9.6 %collective-permute-start.3 = (f32[9,16,512]{2,1,0:T(8,128)S(1)}, f32[9,16,512]{2,1,0:T(8,128)S(1)}, u32[]{:S(2)}, u32[]{:S(2)}) collective-permute-start(f32[9,16,512]{2,1,0:T(8,128)S(1)} %get-tuple-element.53), channel_id=1, source_target_pairs={{0,4},{4,12},{12,8},{8,16},{16,20},{20,28},{28,24},{24,25},{25,29}... | collective-permute-start | bytes 884744 | tf_op jit(solution)/shard_map/ppermute | solution.py:600
  468.4 6.7 %collective-permute-done.2.above_ref = f32[9,16,512]{2,1,0:T(8,128)S(1)} collective-permute-done((f32[9,16,512]{2,1,0:T(8,128)S(1)}, f32[9,16,512]{2,1,0:T(8,128)S(1)}, u32[]{:S(2)}, u32[]{:S(2)}) %collective-permute-start.2) | collective-permute-done | bytes 294944 | tf_op jit(solution)/shard_map/ppermute | solution.py:601
  475.1 10.1 %sweep_solve.7 = (f32[81,16,512]{2,1,0:T(8,128)}, f32[9,64,512]{2,1,0:T(8,128)S(1)}, f32[9,16,512]{2,1,0:T(8,128)S(1)}, f32[9,16,512]{2,1,0:T(8,128)S(1)}) custom-call(f32[9,9]{1,0:T(8,128)S(1)} %copy-done.13, s32[1,512]{1,0:T(1,128)S(1)} %bitcast.22, f32[81,16,512]{2,1,0:T(8,128)} %copy-done.2, f32[81,16,512]{2,1,0:T(8,128)} %get-tuple-element.50.v_ref, ...), custom_call_target="tpu_custom_call" | custom-call | flops 398131200 | bytes 11718980 | tf_op jit(solution)/shard_map/sweep_solve/pallas_call | solution.py:569
  485.2 1.9 collective-permute-start.4
  487.2 4.7 collective-permute-done.4.above_ref
  491.9 11.0 %collective-permute-done.5.below_ref = f32[9,16,512]{2,1,0:T(8,128)S(1)} collective-permute-done((f32[9,16,512]{2,1,0:T(8,128)S(1)}, f32[9,16,512]{2,1,0:T(8,128)S(1)}, u32[]{:S(2)}, u32[]{:S(2)}) %collective-permute-start.5) | collective-permute-done | bytes 294944 | tf_op jit(solution)/shard_map/ppermute | solution.py:600
  502.9 16.9 %finish_solve.3 = f32[8,648,128]{2,1,0:T(8,128)S(1)} custom-call(f32[9,9]{1,0:T(8,128)S(1)} %copy-done.13, s32[1,512]{1,0:T(1,128)S(1)} %bitcast.23, f32[81,16,512]{2,1,0:T(8,128)} %copy-done.2, f32[81,16,512]{2,1,0:T(8,128)} %get-tuple-element.54.v_ref, f32[81,1,512]{2,1,0:T(1,128)S(1)} %get-tuple-element.85.diag_ref, bf16[96,256]{1,0:T(8,128)(2,1)S(1)} %copy-done.11, ...), custom_call_target="tpu_custom_call" | custom-call | flops 2436562944 | bytes 10998084 | tf_op jit(solution)/shard_map/finish_solve/pallas_call | solution.py:569
  519.9 1.5 copy-done.7
  521.4 11.2 %all-to-all-start.1 = ((f32[8,648,128]{2,1,0:T(8,128)}), f32[8,648,128]{2,1,0:T(8,128)}, u32[]{:S(2)}, u32[]{:S(2)}) async-start(f32[8,648,128]{2,1,0:T(8,128)} %copy-done.7), calls=%async_computation.1 | async-start | bytes 5308416 | tf_op jit(solution)/shard_map/all_to_all | solution.py:669
  532.5 7.4 %unpacked.3.refs_0_ = f32[81,3,64,128]{3,2,1,0:T(8,128)} custom-call(f32[8,648,128]{2,1,0:T(8,128)} %all-to-all-done.5.recv_ref, bf16[256,128]{1,0:T(8,128)(2,1)S(1)} %copy-done.14), custom_call_target="tpu_custom_call" | custom-call | flops 339738624 | bytes 5308416 | tf_op jit(solution)/shard_map/unpacked/pallas_call | solution.py:287
  539.9 6.1 %unpacked.4.refs_0_ = f32[81,3,64,128]{3,2,1,0:T(8,128)} custom-call(f32[8,648,128]{2,1,0:T(8,128)S(1)} %all-to-all-done.3.recv_ref, bf16[256,128]{1,0:T(8,128)(2,1)S(1)} %copy-done.14, f32[81,3,64,128]{3,2,1,0:T(8,128)} %unpacked.3.refs_0_), custom_call_target="tpu_custom_call", output_to_operand_aliasing={{}: (2, {})} | custom-call | flops 339738624 | bytes 5308416 | tf_op jit(solution)/shard_map/unpacked/pallas_call | solution.py:287
  546.0 46.4 %all-to-all-done.1.recv_ref = f32[8,648,128]{2,1,0:T(8,128)} async-done(((f32[8,648,128]{2,1,0:T(8,128)}), f32[8,648,128]{2,1,0:T(8,128)}, u32[]{:S(2)}, u32[]{:S(2)}) %all-to-all-start.1) | async-done | bytes 2654240 | tf_op jit(solution)/shard_map/all_to_all | solution.py:669
  592.4 7.4 %unpacked.5 = f32[81,3,64,128]{3,2,1,0:T(8,128)} custom-call(f32[8,648,128]{2,1,0:T(8,128)} %all-to-all-done.1.recv_ref, bf16[256,128]{1,0:T(8,128)(2,1)S(1)} %copy-done.14, f32[81,3,64,128]{3,2,1,0:T(8,128)} %unpacked.4.refs_0_), custom_call_target="tpu_custom_call", output_to_operand_aliasing={{}: (2, {})} | custom-call | flops 339738624 | bytes 5308416 | tf_op jit(solution)/shard_map/unpacked/pallas_call | solution.py:287
  (77 shorter events, 10.7 us)
Async XLA Ops:
  0.0 184.8 %copy-start = (s32[256]{0:T(256)S(1)}, s32[256]{0:T(256)}, u32[]{:S(2)}) copy-start(s32[256]{0:T(256)} %param.15) | copy-start | bytes 3076
  6.8 0.8 copy-start.15
  7.7 0.7 copy-start.23
  17.2 7.4 %copy-start.16 = (bf16[128,256]{1,0:T(8,128)(2,1)S(1)}, bf16[128,256]{1,0:T(8,128)(2,1)}, u32[]{:S(2)}) copy-start(bf16[128,256]{1,0:T(8,128)(2,1)} %get-tuple-element.44.perm_ref) | copy-start | bytes 196612
  17.2 7.4 %copy-start.24 = (f32[3]{0:T(128)S(1)}, f32[3]{0:T(128)}, u32[]{:S(2)}) copy-start(f32[3]{0:T(128)} %dref_ref.5) | copy-start | bytes 40
  17.2 67.6 %all-to-all-start = ((f32[8,648,128]{2,1,0:T(8,128)}), f32[8,648,128]{2,1,0:T(8,128)S(1)}, u32[]{:S(2)}, u32[]{:S(2)}) async-start(f32[8,648,128]{2,1,0:T(8,128)} %packed_source.3), calls=%async_computation | async-start | bytes 5308416 | tf_op jit(solution)/shard_map/all_to_all | solution.py:651
  84.7 1.5 copy-start.25
  86.2 64.1 %all-to-all-start.2 = ((f32[8,648,128]{2,1,0:T(8,128)}), f32[8,648,128]{2,1,0:T(8,128)}, u32[]{:S(2)}, u32[]{:S(2)}) async-start(f32[8,648,128]{2,1,0:T(8,128)} %packed_source.4), calls=%async_computation.2 | async-start | bytes 5308416 | tf_op jit(solution)/shard_map/all_to_all | solution.py:651
  99.6 54.5 %copy-start.27 = (f32[9]{0:T(128)S(1)}, f32[9]{0:T(128)}, u32[]{:S(2)}) copy-start(f32[9]{0:T(128)} %param.13) | copy-start | bytes 112
  150.3 119.4 %all-to-all-start.4 = ((f32[8,648,128]{2,1,0:T(8,128)}), f32[8,648,128]{2,1,0:T(8,128)S(1)}, u32[]{:S(2)}, u32[]{:S(2)}) async-start(f32[8,648,128]{2,1,0:T(8,128)} %packed_source.5), calls=%async_computation.4 | async-start | bytes 5308416 | tf_op jit(solution)/shard_map/all_to_all | solution.py:651
  154.0 11.3 %copy-start.11 = (bf16[96,256]{1,0:T(8,128)(2,1)S(1)}, bf16[96,256]{1,0:T(8,128)(2,1)}, u32[]{:S(2)}) copy-start(bf16[96,256]{1,0:T(8,128)(2,1)} %get-tuple-element.45.link_ref) | copy-start | bytes 147460
  154.0 11.3 %copy-start.13 = (f32[9,9]{1,0:T(8,128)S(1)}, f32[9,9]{1,0:T(8,128)}, u32[]{:S(2)}) copy-start(f32[9,9]{1,0:T(8,128)} %basis_ref.23) | copy-start | bytes 976
  165.2 16.1 %copy-start.17 = (bf16[512,512]{1,0:T(8,128)(2,1)}, bf16[512,512]{1,0:T(8,128)(2,1)S(1)}, u32[]{:S(2)}) copy-start(bf16[512,512]{1,0:T(8,128)(2,1)S(1)} %get-tuple-element.88.rest_ref) | copy-start | bytes 1572868
  165.2 16.1 %copy-start.20 = (bf16[512,512]{1,0:T(8,128)(2,1)}, bf16[512,512]{1,0:T(8,128)(2,1)S(1)}, u32[]{:S(2)}) copy-start(bf16[512,512]{1,0:T(8,128)(2,1)S(1)} %get-tuple-element.89.top_ref) | copy-start | bytes 1572868
  165.2 86.0 %copy-start.8 = (bf16[512,512]{1,0:T(8,128)(2,1)}, bf16[512,512]{1,0:T(8,128)(2,1)S(1)}, u32[]{:S(2)}) copy-start(bf16[512,512]{1,0:T(8,128)(2,1)S(1)} %get-tuple-element.87.top_ref) | copy-start | bytes 1572868
  181.3 1.5 copy-start.3
  182.8 16.8 %collective-permute-start.6 = (f32[9,16,512]{2,1,0:T(8,128)S(1)}, f32[9,16,512]{2,1,0:T(8,128)S(1)}, u32[]{:S(2)}, u32[]{:S(2)}) collective-permute-start(f32[9,16,512]{2,1,0:T(8,128)S(1)} %get-tuple-element.61), channel_id=1, source_target_pairs={{0,3},{4,0},{12,4},{8,12},{16,8},{20,16},{28,20},{24,28},{25,24},{... | collective-permute-start | bytes 884744 | tf_op jit(solution)/shard_map/ppermute | solution.py:601
  183.7 16.0 %collective-permute-start.7 = (f32[9,16,512]{2,1,0:T(8,128)S(1)}, f32[9,16,512]{2,1,0:T(8,128)S(1)}, u32[]{:S(2)}, u32[]{:S(2)}) collective-permute-start(f32[9,16,512]{2,1,0:T(8,128)S(1)} %get-tuple-element.62), channel_id=1, source_target_pairs={{0,4},{4,12},{12,8},{8,16},{16,20},{20,28},{28,24},{24,25},{25,29}... | collective-permute-start | bytes 884744 | tf_op jit(solution)/shard_map/ppermute | solution.py:600
  209.7 12.0 %collective-permute-start.8 = (f32[9,16,512]{2,1,0:T(8,128)S(1)}, f32[9,16,512]{2,1,0:T(8,128)S(1)}, u32[]{:S(2)}, u32[]{:S(2)}) collective-permute-start(f32[9,16,512]{2,1,0:T(8,128)S(1)} %get-tuple-element.65), channel_id=1, source_target_pairs={{0,3},{4,0},{12,4},{8,12},{16,8},{20,16},{28,20},{24,28},{25,24},{... | collective-permute-start | bytes 884744 | tf_op jit(solution)/shard_map/ppermute | solution.py:601
  210.9 10.7 %collective-permute-start.9 = (f32[9,16,512]{2,1,0:T(8,128)S(1)}, f32[9,16,512]{2,1,0:T(8,128)S(1)}, u32[]{:S(2)}, u32[]{:S(2)}) collective-permute-start(f32[9,16,512]{2,1,0:T(8,128)S(1)} %get-tuple-element.66), channel_id=1, source_target_pairs={{0,4},{4,12},{12,8},{8,16},{16,20},{20,28},{28,24},{24,25},{25,29}... | collective-permute-start | bytes 884744 | tf_op jit(solution)/shard_map/ppermute | solution.py:600
  231.8 8.0 %collective-permute-start.10 = (f32[9,16,512]{2,1,0:T(8,128)S(1)}, f32[9,16,512]{2,1,0:T(8,128)S(1)}, u32[]{:S(2)}, u32[]{:S(2)}) collective-permute-start(f32[9,16,512]{2,1,0:T(8,128)S(1)} %get-tuple-element.69), channel_id=1, source_target_pairs={{0,3},{4,0},{12,4},{8,12},{16,8},{20,16},{28,20},{24,28},{25,24},{... | collective-permute-start | bytes 884744 | tf_op jit(solution)/shard_map/ppermute | solution.py:601
  234.7 16.5 %collective-permute-start.11 = (f32[9,16,512]{2,1,0:T(8,128)S(1)}, f32[9,16,512]{2,1,0:T(8,128)S(1)}, u32[]{:S(2)}, u32[]{:S(2)}) collective-permute-start(f32[9,16,512]{2,1,0:T(8,128)S(1)} %get-tuple-element.70), channel_id=1, source_target_pairs={{0,4},{4,12},{12,8},{8,16},{16,20},{20,28},{28,24},{24,25},{25,29}... | collective-permute-start | bytes 884744 | tf_op jit(solution)/shard_map/ppermute | solution.py:600
  268.2 1.5 copy-start.6
  269.7 1.5 copy-start.26
  271.2 124.8 %all-to-all-start.3 = ((f32[8,648,128]{2,1,0:T(8,128)}), f32[8,648,128]{2,1,0:T(8,128)S(1)}, u32[]{:S(2)}, u32[]{:S(2)}) async-start(f32[8,648,128]{2,1,0:T(8,128)} %copy-done.6), calls=%async_computation.3 | async-start | bytes 5308416 | tf_op jit(solution)/shard_map/all_to_all | solution.py:669
  281.9 0.9 copy-start.12
  282.8 1.0 copy-start.18
  283.9 1.0 copy-start.21
  300.4 1.5 copy-start.4
  301.9 22.0 %collective-permute-start.12 = (f32[9,16,512]{2,1,0:T(8,128)S(1)}, f32[9,16,512]{2,1,0:T(8,128)S(1)}, u32[]{:S(2)}, u32[]{:S(2)}) collective-permute-start(f32[9,16,512]{2,1,0:T(8,128)S(1)} %get-tuple-element.73), channel_id=1, source_target_pairs={{0,3},{4,0},{12,4},{8,12},{16,8},{20,16},{28,20},{24,28},{25,24},{... | collective-permute-start | bytes 884744 | tf_op jit(solution)/shard_map/ppermute | solution.py:601
  302.0 22.0 %collective-permute-start.13 = (f32[9,16,512]{2,1,0:T(8,128)S(1)}, f32[9,16,512]{2,1,0:T(8,128)S(1)}, u32[]{:S(2)}, u32[]{:S(2)}) collective-permute-start(f32[9,16,512]{2,1,0:T(8,128)S(1)} %get-tuple-element.74), channel_id=1, source_target_pairs={{0,4},{4,12},{12,8},{8,16},{16,20},{20,28},{28,24},{24,25},{25,29}... | collective-permute-start | bytes 884744 | tf_op jit(solution)/shard_map/ppermute | solution.py:600
  334.0 16.0 %collective-permute-start.14 = (f32[9,16,512]{2,1,0:T(8,128)S(1)}, f32[9,16,512]{2,1,0:T(8,128)S(1)}, u32[]{:S(2)}, u32[]{:S(2)}) collective-permute-start(f32[9,16,512]{2,1,0:T(8,128)S(1)} %get-tuple-element.77), channel_id=1, source_target_pairs={{0,3},{4,0},{12,4},{8,12},{16,8},{20,16},{28,20},{24,28},{25,24},{... | collective-permute-start | bytes 884744 | tf_op jit(solution)/shard_map/ppermute | solution.py:601
  335.2 14.8 %collective-permute-start.15 = (f32[9,16,512]{2,1,0:T(8,128)S(1)}, f32[9,16,512]{2,1,0:T(8,128)S(1)}, u32[]{:S(2)}, u32[]{:S(2)}) collective-permute-start(f32[9,16,512]{2,1,0:T(8,128)S(1)} %get-tuple-element.78), channel_id=1, source_target_pairs={{0,4},{4,12},{12,8},{8,16},{16,20},{20,28},{28,24},{24,25},{25,29}... | collective-permute-start | bytes 884744 | tf_op jit(solution)/shard_map/ppermute | solution.py:600
  350.0 27.5 %copy-start.9 = (bf16[512,512]{1,0:T(8,128)(2,1)S(1)}, bf16[512,512]{1,0:T(8,128)(2,1)}, u32[]{:S(2)}) copy-start(bf16[512,512]{1,0:T(8,128)(2,1)} %copy-done.8) | copy-start | bytes 1572868
  360.2 6.7 %collective-permute-start.16 = (f32[9,16,512]{2,1,0:T(8,128)S(1)}, f32[9,16,512]{2,1,0:T(8,128)S(1)}, u32[]{:S(2)}, u32[]{:S(2)}) collective-permute-start(f32[9,16,512]{2,1,0:T(8,128)S(1)} %get-tuple-element.81), channel_id=1, source_target_pairs={{0,3},{4,0},{12,4},{8,12},{16,8},{20,16},{28,20},{24,28},{25,24},{... | collective-permute-start | bytes 884744 | tf_op jit(solution)/shard_map/ppermute | solution.py:601
  361.8 15.7 %collective-permute-start.17 = (f32[9,16,512]{2,1,0:T(8,128)S(1)}, f32[9,16,512]{2,1,0:T(8,128)S(1)}, u32[]{:S(2)}, u32[]{:S(2)}) collective-permute-start(f32[9,16,512]{2,1,0:T(8,128)S(1)} %get-tuple-element.82), channel_id=1, source_target_pairs={{0,4},{4,12},{12,8},{8,16},{16,20},{20,28},{28,24},{24,25},{25,29}... | collective-permute-start | bytes 884744 | tf_op jit(solution)/shard_map/ppermute | solution.py:600
  394.4 1.6 copy-start.5
  396.0 125.4 %all-to-all-start.5 = ((f32[8,648,128]{2,1,0:T(8,128)}), f32[8,648,128]{2,1,0:T(8,128)}, u32[]{:S(2)}, u32[]{:S(2)}) async-start(f32[8,648,128]{2,1,0:T(8,128)} %copy-done.5), calls=%async_computation.5 | async-start | bytes 5308416 | tf_op jit(solution)/shard_map/all_to_all | solution.py:669
  407.2 1.0 copy-start.19
  408.2 1.0 copy-start.22
  424.7 1.5 copy-start.2
  426.3 19.5 %collective-permute-start = (f32[9,16,512]{2,1,0:T(8,128)S(1)}, f32[9,16,512]{2,1,0:T(8,128)S(1)}, u32[]{:S(2)}, u32[]{:S(2)}) collective-permute-start(f32[9,16,512]{2,1,0:T(8,128)S(1)} %get-tuple-element.48), channel_id=1, source_target_pairs={{0,3},{4,0},{12,4},{8,12},{16,8},{20,16},{28,20},{24,28},{25,24},{... | collective-permute-start | bytes 884744 | tf_op jit(solution)/shard_map/ppermute | solution.py:601
  426.4 19.4 %collective-permute-start.1 = (f32[9,16,512]{2,1,0:T(8,128)S(1)}, f32[9,16,512]{2,1,0:T(8,128)S(1)}, u32[]{:S(2)}, u32[]{:S(2)}) collective-permute-start(f32[9,16,512]{2,1,0:T(8,128)S(1)} %get-tuple-element.49), channel_id=1, source_target_pairs={{0,4},{4,12},{12,8},{8,16},{16,20},{20,28},{28,24},{24,25},{25,29}... | collective-permute-start | bytes 884744 | tf_op jit(solution)/shard_map/ppermute | solution.py:600
  455.9 19.2 %collective-permute-start.2 = (f32[9,16,512]{2,1,0:T(8,128)S(1)}, f32[9,16,512]{2,1,0:T(8,128)S(1)}, u32[]{:S(2)}, u32[]{:S(2)}) collective-permute-start(f32[9,16,512]{2,1,0:T(8,128)S(1)} %get-tuple-element.52), channel_id=1, source_target_pairs={{0,3},{4,0},{12,4},{8,12},{16,8},{20,16},{28,20},{24,28},{25,24},{... | collective-permute-start | bytes 884744 | tf_op jit(solution)/shard_map/ppermute | solution.py:601
  458.8 16.3 %collective-permute-start.3 = (f32[9,16,512]{2,1,0:T(8,128)S(1)}, f32[9,16,512]{2,1,0:T(8,128)S(1)}, u32[]{:S(2)}, u32[]{:S(2)}) collective-permute-start(f32[9,16,512]{2,1,0:T(8,128)S(1)} %get-tuple-element.53), channel_id=1, source_target_pairs={{0,4},{4,12},{12,8},{8,16},{16,20},{20,28},{28,24},{24,25},{25,29}... | collective-permute-start | bytes 884744 | tf_op jit(solution)/shard_map/ppermute | solution.py:600
  475.1 27.8 %copy-start.10 = (bf16[512,512]{1,0:T(8,128)(2,1)S(1)}, bf16[512,512]{1,0:T(8,128)(2,1)}, u32[]{:S(2)}) copy-start(bf16[512,512]{1,0:T(8,128)(2,1)} %copy-done.8) | copy-start | bytes 1572868
  485.2 6.7 %collective-permute-start.4 = (f32[9,16,512]{2,1,0:T(8,128)S(1)}, f32[9,16,512]{2,1,0:T(8,128)S(1)}, u32[]{:S(2)}, u32[]{:S(2)}) collective-permute-start(f32[9,16,512]{2,1,0:T(8,128)S(1)} %get-tuple-element.56), channel_id=1, source_target_pairs={{0,3},{4,0},{12,4},{8,12},{16,8},{20,16},{28,20},{24,28},{25,24},{... | collective-permute-start | bytes 884744 | tf_op jit(solution)/shard_map/ppermute | solution.py:601
  487.1 15.8 %collective-permute-start.5 = (f32[9,16,512]{2,1,0:T(8,128)S(1)}, f32[9,16,512]{2,1,0:T(8,128)S(1)}, u32[]{:S(2)}, u32[]{:S(2)}) collective-permute-start(f32[9,16,512]{2,1,0:T(8,128)S(1)} %get-tuple-element.57), channel_id=1, source_target_pairs={{0,4},{4,12},{12,8},{8,16},{16,20},{20,28},{28,24},{24,25},{25,29}... | collective-permute-start | bytes 884744 | tf_op jit(solution)/shard_map/ppermute | solution.py:600
  519.8 1.5 copy-start.7
  521.4 11.2 %copy-start.14 = (bf16[256,128]{1,0:T(8,128)(2,1)S(1)}, bf16[256,128]{1,0:T(8,128)(2,1)}, u32[]{:S(2)}) copy-start(bf16[256,128]{1,0:T(8,128)(2,1)} %get-tuple-element.58.perm_ref) | copy-start | bytes 196612
  521.4 71.0 %all-to-all-start.1 = ((f32[8,648,128]{2,1,0:T(8,128)}), f32[8,648,128]{2,1,0:T(8,128)}, u32[]{:S(2)}, u32[]{:S(2)}) async-start(f32[8,648,128]{2,1,0:T(8,128)} %copy-done.7), calls=%async_computation.1 | async-start | bytes 5308416 | tf_op jit(solution)/shard_map/all_to_all | solution.py:669
  592.4 7.4 %copy-start.1 = (s32[256]{0:T(256)S(1)}, s32[256]{0:T(256)}, u32[]{:S(2)}) copy-start(s32[256]{0:T(256)} %param.15) | copy-start | bytes 3076
